TPU v7x, 32 devices: a whole 2x2x4 slice. The times are simulated.
32 devices in a mesh: dp: 4 (over y, core), ctx: 8 (over z, x).
Axes of the slice: x: 2, y: 2, z: 4, core: 2. Of those that a mesh axis runs over, the one named last changes fastest.
Arguments:
- layer_input: bfloat16 [2, 4, 1024, 768], P(None, 'dp', 'ctx'), may hold values from -6 to 6
- doc_lengths: int32 [2, 4, 5], P(None, 'dp'), may hold values from 1 to 1020, as said below
- ln1_gain: float32 [768], replicated, may hold values from 0.5 to 1.5
- ln1_bias: float32 [768], replicated, may hold values from -3 to 3
- w_qkv: bfloat16 [768, 2304], P('dp'), may hold values from -0.21875 to 0.21875
- w_out: bfloat16 [768, 768], P('dp'), may hold values from -1.25 to 1.25
- ln2_gain: float32 [768], replicated, may hold values from 0.5 to 1.5
- ln2_bias: float32 [768], replicated, may hold values from -3 to 3
- w_up: bfloat16 [768, 3072], P('dp'), may hold values from -0.21875 to 0.21875
- b_up: float32 [3072], replicated, may hold values from -3 to 3
- w_down: bfloat16 [3072, 768], P('dp'), may hold values from -0.109375 to 0.109375
- cotangent: bfloat16 [2, 4, 1024, 768], P(None, 'dp', 'ctx'), may hold values from -6 to 6
Outputs:
- layer_output: bfloat16 [2, 4, 1024, 768], P(None, 'dp', 'ctx')
- d_x: bfloat16 [2, 4, 1024, 768], P(None, 'dp', 'ctx')
- d_ln1_gain: float32 [768], replicated
- d_ln1_bias: float32 [768], replicated
- d_w_qkv: float32 [768, 2304], P('dp', 'ctx')
- d_w_out: float32 [768, 768], P('dp', 'ctx')
- d_ln2_gain: float32 [768], replicated
- d_ln2_bias: float32 [768], replicated
- d_w_up: float32 [768, 3072], P('dp', 'ctx')
- d_b_up: float32 [3072], replicated
- d_w_down: float32 [3072, 768], P('dp', 'ctx')
Inputs may be any that keep to these rules, and one draw needn't show every extreme that they name: `doc_lengths`: each row packs 5 documents in order: a first one shorter than 128 tokens, a second one that ends within the last 128 positions of the row, then 5 - 2 documents of at most 32 tokens each; positions after their sum are padding. Some row of each draw has padding of zero length.
All inputs are finite; a program needn't handle non-finite values.
Results may differ from a plain program's by a relative error of at most 0.014.
Values may be sent and summed in bfloat16 or wider, within the bound.
A program may use at most 256 MiB of HBM per device.

v0:
```python
import math
from functools import partial
from types import SimpleNamespace

import jax
import jax.numpy as jnp
from jax import lax
from jax.experimental import pallas as pl
from jax.experimental.pallas import tpu as pltpu
from jax.sharding import PartitionSpec as P

HD = 64


NORM_EPSILON = 1e-05
MASKED = -1e30
START_TOP = -1e20


def prefix_2(array, axis, combine, identity, reverse):
    peers, index = (lax.axis_size(axis), lax.axis_index(axis))
    everything = lax.all_gather(array, axis)
    start = jnp.broadcast_to(jnp.asarray(identity, array.dtype), array.shape)

    def turn(k, before):
        at = peers - 1 - k if reverse else k
        reached = at > index if reverse else at < index
        new = combine(before, everything[at])
        return jnp.where(reached, new, before)

    return lax.fori_loop(0, peers, turn, start)


def layer_norm(value, gain, bias):
    row_mean = jnp.mean(value, axis=-1, keepdims=True)
    centered = value - row_mean
    spread = jnp.mean(centered * centered, axis=-1, keepdims=True)
    return centered * lax.rsqrt(spread + NORM_EPSILON) * gain + bias


def matmul(left, right):
    return jnp.dot(left, right, preferred_element_type=jnp.float32)


def contract_rows(left, right):
    return lax.dot_general(
        left, right, (((0,), (0,)), ((), ())), preferred_element_type=jnp.float32
    )


def contract_cols(left, right):
    return lax.dot_general(
        left, right, (((1,), (1,)), ((), ())), preferred_element_type=jnp.float32
    )


def segment_table(lengths, row_length):
    doc_ends = jnp.cumsum(lengths)
    places = jnp.arange(row_length, dtype=jnp.int32)
    segment = jnp.sum((places[:, None] >= doc_ends[None, :]).astype(jnp.int32), axis=1)
    opening = jnp.concatenate([jnp.ones((1,), jnp.bool_), segment[1:] != segment[:-1]])
    return (segment, opening)


def add_up(earlier, later):
    return earlier + later


def per_token_device(
    layer_input,
    doc_lengths,
    ln1_gain,
    ln1_bias,
    w_qkv,
    w_out,
    ln2_gain,
    ln2_bias,
    w_up,
    b_up,
    w_down,
    cotangent,
):
    micro_count = layer_input.shape[0]
    query_rows = layer_input.shape[2]
    model_width = layer_input.shape[3]
    head_count = model_width // HD
    row_length = query_rows * lax.axis_size("ctx")
    key_block = min(512, row_length)
    score_scale = HD ** (-0.5)
    strength = 8.0 / row_length
    ctx_place = lax.axis_index("ctx")
    query_pos = ctx_place * query_rows + jnp.arange(query_rows, dtype=jnp.int32)
    block_total = ((ctx_place + 1) * query_rows + key_block - 1) // key_block
    later_heads = (jnp.arange(head_count) > 0).astype(jnp.float32)[:, None, None]
    zeros_row = jnp.zeros((row_length,), jnp.float32)
    gelu_exact = partial(jax.nn.gelu, approximate=False)
    output_list = []
    input_grads = []
    matrix_total = None
    vector_total = None
    for micro_step in range(micro_count):
        w_qkv_all, w_out_all, w_up_all, w_down_all = (
            lax.all_gather(w_qkv, "dp", axis=0, tiled=True),
            lax.all_gather(w_out, "dp", axis=0, tiled=True),
            lax.all_gather(w_up, "dp", axis=0, tiled=True),
            lax.all_gather(w_down, "dp", axis=0, tiled=True),
        )
        inputs = layer_input[micro_step, 0].astype(jnp.float32)
        segment, opening = segment_table(doc_lengths[micro_step, 0], row_length)
        query_seg = lax.dynamic_slice_in_dim(segment, ctx_place * query_rows, query_rows, 0)
        normed_one = layer_norm(inputs, ln1_gain, ln1_bias).astype(jnp.bfloat16)
        projected = matmul(normed_one, w_qkv_all).astype(jnp.bfloat16)
        queries = projected[:, :model_width]
        queries3 = queries.reshape(query_rows, head_count, HD)
        query_zero = queries[:, :HD]
        keys_all, values_all = (
            lax.all_gather(projected[:, model_width : 2 * model_width], "ctx", axis=0, tiled=True),
            lax.all_gather(projected[:, 2 * model_width :], "ctx", axis=0, tiled=True),
        )

        def masks(key_start):
            key_seg = lax.dynamic_slice_in_dim(segment, key_start, key_block, 0)
            key_open = lax.dynamic_slice_in_dim(opening, key_start, key_block, 0)
            key_pos = key_start + jnp.arange(key_block, dtype=jnp.int32)
            same_doc = query_seg[:, None] == key_seg[None, :]
            allowed = same_doc & (key_pos[None, :] <= query_pos[:, None])
            chosen = (
                same_doc
                & (key_pos[None, :] < query_pos[:, None])
                & jnp.logical_not(key_open)[None, :]
            )
            return (allowed, chosen.astype(jnp.float32))

        def head_scores(key_start):
            key_zero = lax.dynamic_slice_in_dim(keys_all, key_start, key_block, 0)[:, :HD]
            return (key_zero, contract_cols(query_zero, key_zero) * score_scale)

        def block_keys(key_start):
            keys3 = lax.dynamic_slice_in_dim(keys_all, key_start, key_block, 0).reshape(
                key_block, head_count, HD
            )
            values3 = lax.dynamic_slice_in_dim(values_all, key_start, key_block, 0).reshape(
                key_block, head_count, HD
            )
            return (keys3, values3)

        def logits_of(key_start, keys3):
            allowed, chosen = masks(key_start)
            raw_scores = (
                jnp.einsum("qhd,khd->hqk", queries3, keys3, preferred_element_type=jnp.float32)
                * score_scale
            )
            picked = strength * jax.nn.softplus(raw_scores[0]) * chosen
            before = lax.dynamic_slice_in_dim(prefix, key_start, key_block, 0)
            penalty = before[None, :] + jnp.cumsum(picked, axis=0) - picked
            return jnp.where(allowed[None], raw_scores - penalty[None], MASKED)

        def total_block(block_index, totals):
            key_start = block_index * key_block
            _, chosen = masks(key_start)
            _, first_scores = head_scores(key_start)
            picked = strength * jax.nn.softplus(first_scores) * chosen
            return lax.dynamic_update_slice_in_dim(totals, jnp.sum(picked, axis=0), key_start, 0)

        totals = lax.fori_loop(0, block_total, total_block, zeros_row)
        prefix = prefix_2(totals, "ctx", add_up, zeros_row, False)

        def stat_block(block_index, running):
            row_top, row_total = running
            key_start = block_index * key_block
            keys3, _ = block_keys(key_start)
            logits = logits_of(key_start, keys3)
            new_top = jnp.maximum(row_top, jnp.max(logits, axis=-1))
            row_total = row_total * jnp.exp(row_top - new_top) + jnp.sum(
                jnp.exp(logits - new_top[..., None]), axis=-1
            )
            return (new_top, row_total)

        row_top, row_total = lax.fori_loop(
            0,
            block_total,
            stat_block,
            (
                jnp.full((head_count, query_rows), START_TOP, jnp.float32),
                jnp.zeros((head_count, query_rows), jnp.float32),
            ),
        )
        log_total = row_top + jnp.log(row_total)

        def out_block(block_index, gathered_out):
            key_start = block_index * key_block
            keys3, values3 = block_keys(key_start)
            attn_probs = jnp.exp(logits_of(key_start, keys3) - log_total[..., None]).astype(
                jnp.bfloat16
            )
            return gathered_out + jnp.einsum(
                "hqk,khd->qhd", attn_probs, values3, preferred_element_type=jnp.float32
            )

        gathered_out = lax.fori_loop(
            0, block_total, out_block, jnp.zeros((query_rows, head_count, HD), jnp.float32)
        )
        attended = gathered_out.reshape(query_rows, model_width).astype(jnp.bfloat16)
        mid_stream = inputs + matmul(attended, w_out_all)
        normed_two = layer_norm(mid_stream, ln2_gain, ln2_bias).astype(jnp.bfloat16)
        hidden = matmul(normed_two, w_up_all) + b_up
        activated = gelu_exact(hidden).astype(jnp.bfloat16)
        output_list.append((mid_stream + matmul(activated, w_down_all)).astype(jnp.bfloat16))
        cot_rows = cotangent[micro_step, 0]
        grad_down = contract_rows(activated, cot_rows)
        grad_act = contract_cols(cot_rows, w_down_all)
        _, gelu_back = jax.vjp(gelu_exact, hidden)
        grad_hidden = gelu_back(grad_act)[0].astype(jnp.bfloat16)
        grad_up = contract_rows(normed_two, grad_hidden)
        grad_bias_up = jnp.sum(grad_hidden.astype(jnp.float32), axis=0)
        grad_normed_two = contract_cols(grad_hidden, w_up_all)
        _, norm_two_back = jax.vjp(layer_norm, mid_stream, ln2_gain, ln2_bias)
        grad_mid_part, grad_gain_two, grad_bias_two = norm_two_back(grad_normed_two)
        grad_mid = cot_rows.astype(jnp.float32) + grad_mid_part
        grad_branch = grad_mid.astype(jnp.bfloat16)
        grad_outproj = contract_rows(attended, grad_branch)
        grad_attended = contract_cols(grad_branch, w_out_all).astype(jnp.bfloat16)
        grad_att3 = grad_attended.reshape(query_rows, head_count, HD)
        row_delta = jnp.einsum("qhd,qhd->hq", grad_att3.astype(jnp.float32), gathered_out)

        def grad_block(block_index, running):
            grad_query, grad_key_all, grad_value_all, penalty_grad, first_grad = running
            key_start = block_index * key_block
            keys3, values3 = block_keys(key_start)
            probs_f32 = jnp.exp(logits_of(key_start, keys3) - log_total[..., None])
            grad_probs = jnp.einsum(
                "qhd,khd->hqk", grad_att3, values3, preferred_element_type=jnp.float32
            )
            grad_logits = probs_f32 * (grad_probs - row_delta[..., None])
            penalty_grad = lax.dynamic_update_slice_in_dim(
                penalty_grad, -jnp.sum(grad_logits, axis=0), key_start, 1
            )
            first_grad = lax.dynamic_update_slice_in_dim(first_grad, grad_logits[0], key_start, 1)
            grad_scores = (grad_logits * later_heads).astype(jnp.bfloat16)
            grad_query = (
                grad_query
                + jnp.einsum("hqk,khd->qhd", grad_scores, keys3, preferred_element_type=jnp.float32)
                * score_scale
            )
            key_part = (
                jnp.einsum(
                    "hqk,qhd->khd", grad_scores, queries3, preferred_element_type=jnp.float32
                )
                * score_scale
            )
            value_part = jnp.einsum(
                "hqk,qhd->khd",
                probs_f32.astype(jnp.bfloat16),
                grad_att3,
                preferred_element_type=jnp.float32,
            )
            grad_key_all = lax.dynamic_update_slice_in_dim(
                grad_key_all, key_part.reshape(key_block, model_width), key_start, 0
            )
            grad_value_all = lax.dynamic_update_slice_in_dim(
                grad_value_all, value_part.reshape(key_block, model_width), key_start, 0
            )
            return (grad_query, grad_key_all, grad_value_all, penalty_grad, first_grad)

        grad_query, grad_key_all, grad_value_all, penalty_grad, first_grad = lax.fori_loop(
            0,
            block_total,
            grad_block,
            (
                jnp.zeros((query_rows, head_count, HD), jnp.float32),
                jnp.zeros((row_length, model_width), jnp.float32),
                jnp.zeros((row_length, model_width), jnp.float32),
                jnp.zeros((query_rows, row_length), jnp.float32),
                jnp.zeros((query_rows, row_length), jnp.float32),
            ),
        )
        column_sums = jnp.sum(penalty_grad, axis=0)
        after = prefix_2(column_sums, "ctx", add_up, zeros_row, True)
        reach_sums = after + column_sums

        def head_block(block_index, running):
            grad_query_zero, grad_key_all = running
            key_start = block_index * key_block
            _, chosen = masks(key_start)
            key_zero, first_scores = head_scores(key_start)
            flow_block = lax.dynamic_slice_in_dim(penalty_grad, key_start, key_block, 1)
            reach_block = lax.dynamic_slice_in_dim(reach_sums, key_start, key_block, 0)
            grad_picked = reach_block[None, :] - jnp.cumsum(flow_block, axis=0)
            grad_select = grad_picked * strength * jax.nn.sigmoid(first_scores) * chosen
            grad_head = (
                lax.dynamic_slice_in_dim(first_grad, key_start, key_block, 1) + grad_select
            ).astype(jnp.bfloat16)
            grad_query_zero = grad_query_zero + matmul(grad_head, key_zero) * score_scale
            key_zero_grad = contract_rows(grad_head, query_zero) * score_scale
            grad_key_all = lax.dynamic_update_slice(
                grad_key_all, key_zero_grad, (key_start, jnp.zeros((), jnp.int32))
            )
            return (grad_query_zero, grad_key_all)

        grad_query_zero, grad_key_all = lax.fori_loop(
            0, block_total, head_block, (jnp.zeros((query_rows, HD), jnp.float32), grad_key_all)
        )
        grad_query = grad_query.at[:, 0, :].add(grad_query_zero).reshape(query_rows, model_width)
        grad_key_own, grad_value_own = (
            lax.psum_scatter(grad_key_all, "ctx", scatter_dimension=0, tiled=True),
            lax.psum_scatter(grad_value_all, "ctx", scatter_dimension=0, tiled=True),
        )
        grad_project = jnp.concatenate([grad_query, grad_key_own, grad_value_own], axis=1).astype(
            jnp.bfloat16
        )
        grad_qkv = contract_rows(normed_one, grad_project)
        grad_normed_one = contract_cols(grad_project, w_qkv_all)
        _, norm_one_back = jax.vjp(layer_norm, inputs, ln1_gain, ln1_bias)
        grad_in_part, grad_gain_one, grad_bias_one = norm_one_back(grad_normed_one)
        input_grads.append((grad_mid + grad_in_part).astype(jnp.bfloat16))
        matrix_grads = (grad_qkv, grad_outproj, grad_up, grad_down)
        vector_grads = (grad_gain_one, grad_bias_one, grad_gain_two, grad_bias_two, grad_bias_up)
        matrix_grads = (
            lax.psum_scatter(matrix_grads[0], "ctx", scatter_dimension=1, tiled=True),
            lax.psum_scatter(matrix_grads[1], "ctx", scatter_dimension=1, tiled=True),
            lax.psum_scatter(matrix_grads[2], "ctx", scatter_dimension=1, tiled=True),
            lax.psum_scatter(matrix_grads[3], "ctx", scatter_dimension=1, tiled=True),
        )
        matrix_grads = (
            lax.psum_scatter(
                matrix_grads[0].astype(jnp.bfloat16), "dp", scatter_dimension=0, tiled=True
            ).astype(jnp.float32),
            lax.psum_scatter(
                matrix_grads[1].astype(jnp.bfloat16), "dp", scatter_dimension=0, tiled=True
            ).astype(jnp.float32),
            lax.psum_scatter(
                matrix_grads[2].astype(jnp.bfloat16), "dp", scatter_dimension=0, tiled=True
            ).astype(jnp.float32),
            lax.psum_scatter(
                matrix_grads[3].astype(jnp.bfloat16), "dp", scatter_dimension=0, tiled=True
            ).astype(jnp.float32),
        )
        vector_grads = lax.psum(
            (vector_grads[0], vector_grads[1], vector_grads[2], vector_grads[3], vector_grads[4]),
            ("dp", "ctx"),
        )
        if matrix_total is None:
            matrix_total = matrix_grads
            vector_total = vector_grads
        else:
            matrix_total = tuple((old + new for old, new in zip(matrix_total, matrix_grads)))
            vector_total = tuple((old + new for old, new in zip(vector_total, vector_grads)))
    layer_out = jnp.stack(output_list)[:, None]
    input_out = jnp.stack(input_grads)[:, None]
    return (
        layer_out,
        input_out,
        vector_total[0],
        vector_total[1],
        matrix_total[0],
        matrix_total[1],
        vector_total[2],
        vector_total[3],
        matrix_total[2],
        vector_total[4],
        matrix_total[3],
    )


MESH = pl.DeviceIdType.MESH
EXCLUDED = 1e30
QUERY_BLOCK = 256


def norm_parts(value):
    row_mean = jnp.mean(value, axis=-1, keepdims=True)
    centered = value - row_mean
    spread = jnp.mean(centered * centered, axis=-1, keepdims=True)
    inverse = lax.rsqrt(spread + NORM_EPSILON)
    return centered * inverse, inverse


def norm_back(xhat, inverse, grad, gain):
    scaled = grad * gain
    return (
        scaled
        - jnp.mean(scaled, axis=-1, keepdims=True)
        - xhat * jnp.mean(scaled * xhat, axis=-1, keepdims=True)
    ) * inverse


class Wires:
    def __init__(self, send_sem, recv_sem):
        self.send_sem, self.recv_sem, self.used, self.made = send_sem, recv_sem, 0, []

    def send(self, source, target, where):
        copy = pltpu.make_async_remote_copy(
            src_ref=source,
            dst_ref=target,
            send_sem=self.send_sem.at[self.used],
            recv_sem=self.recv_sem.at[self.used],
            device_id=where,
            device_id_type=MESH,
        )
        copy.start()
        self.used += 1
        self.made.append(copy)
        return copy

    def later(self, source, target, where):
        copy = pltpu.make_async_remote_copy(
            src_ref=source,
            dst_ref=target,
            send_sem=self.send_sem.at[self.used],
            recv_sem=self.recv_sem.at[self.used],
            device_id=where,
            device_id_type=MESH,
        )
        self.used += 1
        self.made.append(copy)
        return copy

    def drain(self):
        for copy in self.made:
            copy.wait_send()


def rounded(value):
    return value.astype(jnp.bfloat16)


def folded(array):
    half = array.shape[0] // 2
    return jnp.concatenate([array[:half], array[half:]], axis=1)


def unfolded(array):
    half = array.shape[1] // 2
    return jnp.concatenate([array[:, :half], array[:, half:]], axis=0)


def arrived(like, target, sem):
    pltpu.make_async_copy(like, target, sem).wait()


def swap(index):
    return index + 1 - 2 * lax.rem(index, 2)


def layer_body(plan, loaded, names, lengths, *refs):
    given, refs = refs[: len(loaded)], refs[len(loaded) :]
    r = SimpleNamespace(**dict(zip(names, refs)))
    groups, shards = plan
    f32 = jnp.float32
    ctx, dp = lax.axis_index("ctx"), lax.axis_index("dp")
    ctx_size, tokens, model = r.x_row.shape
    width = r.out.shape[1]
    lines = ctx_size // 2
    mbs = ctx_size // groups
    hpg = width // HD
    own = r.x.shape[0]
    ff = r.w_down.shape[0]
    row_length = tokens * ctx_size
    side, line = lax.rem(ctx, 2), ctx // 2
    my_mb, my_group = ctx // groups, lax.rem(ctx, groups)
    wires = Wires(r.send_sem, r.recv_sem)
    core, far, far_core = {"dp": swap(dp)}, {"dp": lax.rem(dp + 2, 4)}, {"dp": lax.rem(swap(dp) + 2, 4)}
    beside = {"ctx": swap(ctx)}
    up_to = {"dp": lax.rem(ctx, 4), "ctx": shards * dp + ctx // 4}
    up_from = {"dp": ctx // shards, "ctx": lax.rem(ctx, shards) * 4 + dp}
    around = [{"ctx": lax.rem(ctx + step, ctx_size)} for step in range(1, ctx_size)]

    mirror = {"ctx": lax.rem(line + lines // 2, lines) * 2 + side}
    ahead = {"ctx": swap(line) * 2 + side}
    beside_at, mirror_at, ahead_at = beside["ctx"], mirror["ctx"], ahead["ctx"]
    half = tokens // 4

    loads = SimpleNamespace()
    for at, name in enumerate(loaded):
        copy = pltpu.make_async_copy(given[at], getattr(r, name), r.load_sem.at[at])
        copy.start()
        setattr(loads, name, copy)
    barrier = pltpu.get_barrier_semaphore()
    for where in around + [core, far, far_core, up_from]:
        pl.semaphore_signal(barrier, inc=1, device_id=where, device_id_type=MESH)
    loads.x.wait()
    loads.w_qkv.wait()
    pl.semaphore_wait(barrier, ctx_size + 3)

    def x_of(micro):
        return r.x.at[pl.ds(pl.multiple_of(micro * tokens, tokens), tokens)]

    x_mirror = wires.send(x_of(1 - my_mb), r.x_row.at[ctx], mirror)
    x_beside = wires.send(x_of(my_mb), r.x_row.at[ctx], beside)
    x_ahead = wires.send(x_of(my_mb), r.x_row.at[ctx], ahead)
    for group in range(groups):

        @pl.when(my_group == group)
        def _():
            for kind in range(3):
                first = kind * model + group * width
                r.w_pick[dp, :, kind * width : (kind + 1) * width] = r.w_qkv[:, first : first + width]

    for kind in range(2):
        r.w_pick[dp, :, 3 * width + kind * HD : 3 * width + (kind + 1) * HD] = r.w_qkv[
            :, kind * model : kind * model + HD
        ]
    pick_far = wires.send(r.w_pick.at[dp], r.w_pick.at[dp], far)
    pick_core = wires.send(r.w_pick.at[dp], r.w_pick.at[dp], core)
    r.x_row[ctx] = x_of(my_mb)[...]

    for copy in (loads.cot, loads.w_out_own, loads.w_up_own):
        copy.wait()

    def rows_of(place):
        return pl.ds(pl.multiple_of(place * size_dp, size_dp), size_dp)

    size_dp = model // 4
    wout_far = wires.send(r.w_out_own, r.w_out.at[rows_of(dp)], far)
    wout_core = wires.send(r.w_out_own, r.w_out.at[rows_of(dp)], core)

    def up_part(peer):
        return r.w_up_own.at[:, pl.ds(pl.multiple_of(peer * ff, 128), ff)]

    up_in = [
        wires.send(up_part(where["dp"]), r.w_up.at[rows_of(dp)], where)
        for where in (far, far_core, core)
    ]
    cot_far = wires.send(r.cot, r.cots.at[2], far)
    cot_core = wires.send(r.cot, r.cots.at[1], core)
    r.w_out[rows_of(dp), :] = r.w_out_own[...]
    r.w_up[rows_of(dp), :] = up_part(dp)[...]
    r.cots[0] = r.cot[...]

    loads.gain_one.wait()
    loads.bias_one.wait()
    gain_one = r.gain_one[...].reshape(1, model)
    bias_one = r.bias_one[...].reshape(1, model)

    def normalise(place):
        xhat, _ = norm_parts(r.x_row[place].astype(f32))
        rows = pl.ds(pl.multiple_of(place * tokens, tokens), tokens)
        r.hat_one[rows, :] = rounded(xhat)
        r.normed_one[rows, :] = rounded(xhat * gain_one + bias_one)

    x_beside.wait_recv()
    top, bottom = pl.ds(0, half), pl.ds(half, tokens - half)
    x_fwd_a = wires.send(r.x_row.at[beside_at, top], r.x_row.at[beside_at, top], ahead)
    x_ahead.wait_recv()
    x_fwd_b = wires.send(r.x_row.at[ahead_at, bottom], r.x_row.at[ahead_at, bottom], beside)
    normalise(ctx)
    x_mirror.wait_recv()
    x_mirror_beside = wires.send(r.x_row.at[mirror_at], r.x_row.at[mirror_at], beside)
    x_mirror_ahead = wires.send(r.x_row.at[mirror_at], r.x_row.at[mirror_at], ahead)
    pick_far.wait_recv()
    pick_at = far["dp"]
    pick_fwd = wires.send(r.w_pick.at[pick_at], r.w_pick.at[pick_at], core)

    normalise(beside_at)
    normalise(ahead_at)
    normalise(mirror_at)
    x_mirror_beside.wait_recv()
    place = swap(mirror_at)
    x_fwd_c = wires.send(r.x_row.at[place, top], r.x_row.at[place, top], ahead)
    x_mirror_ahead.wait_recv()
    place = lax.rem(ahead_at + ctx_size // 2, ctx_size)
    x_fwd_d = wires.send(r.x_row.at[place, bottom], r.x_row.at[place, bottom], beside)
    normalise(swap(mirror_at))
    normalise(place)
    x_fwd_a.wait_recv()
    x_fwd_b.wait_recv()
    normalise(swap(ahead_at))
    pick_core.wait_recv()
    pick_fwd.wait_recv()
    x_fwd_c.wait_recv()
    x_fwd_d.wait_recv()
    normalise(swap(place))
    w_pick = r.w_pick[...].reshape(model, 3 * width + 2 * HD)
    r.proj[...] = rounded(matmul(r.normed_one[...], w_pick))

    def att_copy(place):
        return pltpu.make_async_remote_copy(
            src_ref=r.att.at[place],
            dst_ref=r.att_in.at[ctx],
            send_sem=r.att_send.at[place],
            recv_sem=r.att_recv.at[ctx],
            device_id={"ctx": place},
            device_id_type=MESH,
        )

    block = QUERY_BLOCK
    per_block = block // tokens
    scale = HD ** (-0.5)
    strength = 8.0 / row_length
    row_at = lax.broadcasted_iota(jnp.int32, (block, block), 0)
    col_at = lax.broadcasted_iota(jnp.int32, (block, block), 1)
    earlier = (col_at < row_at).astype(jnp.bfloat16)
    later = (col_at > row_at).astype(jnp.bfloat16)
    doc_ends, doc_end = [], 0
    for at in range(lengths.shape[2]):
        doc_end = doc_end + lengths[my_mb, 0, at]
        doc_ends.append(doc_end)

    def segment_of(places):
        total = jnp.zeros(places.shape, jnp.int32)
        for end in doc_ends:
            total += jnp.where(places >= end, 1, 0)
        return total

    r.suffix[...] = jnp.zeros_like(r.suffix)
    for start in range(0, row_length, block):
        reach = start + block
        rows = pl.ds(start, block)
        probs_ref, slope_ref = getattr(r, "probs%d" % start), getattr(r, "slope%d" % start)
        row_pos = start + lax.broadcasted_iota(jnp.int32, (block, 1), 0)
        col_pos = lax.broadcasted_iota(jnp.int32, (1, reach), 1)
        row_seg, col_seg = segment_of(row_pos), segment_of(col_pos)
        opening = (col_seg != segment_of(col_pos - 1)) | (col_pos == 0)
        pick_seg = jnp.where(opening, -1, col_seg)
        query = rounded(r.proj[rows, 3 * width : 3 * width + HD] * scale)
        key = r.proj[:reach, 3 * width + HD : 3 * width + 2 * HD]
        scores = contract_cols(query, key)
        small = jnp.exp(-jnp.abs(scores))
        soft = jnp.maximum(scores, 0.0) + jnp.log(1.0 + small)
        recip = 1.0 / (1.0 + small)
        sigmoid = jnp.where(scores >= 0.0, recip, small * recip)
        chosen = (row_seg == pick_seg) & (col_pos < row_pos)
        picked = jnp.where(chosen, strength * soft, 0.0)
        slope_ref[...] = rounded(jnp.where(chosen, strength * sigmoid, 0.0))
        high = rounded(picked)
        low = rounded(picked - high.astype(f32))
        penalty = r.suffix[:, :reach] + (matmul(earlier, high) + matmul(earlier, low))
        allowed = (row_seg == col_seg) & (col_pos <= row_pos)
        penalty = jnp.where(allowed, penalty, EXCLUDED)
        r.suffix[:, :reach] += jnp.sum(picked, axis=0, keepdims=True)
        for head in range(hpg):
            at = head * HD
            query = rounded(r.proj[rows, at : at + HD] * scale)
            key = r.proj[:reach, width + at : width + at + HD]
            value = r.proj[:reach, 2 * width + at : 2 * width + at + HD]
            logits = contract_cols(query, key) - penalty
            top_logit = jnp.max(logits, axis=1, keepdims=True)
            probs = jnp.exp(logits - top_logit)
            inverse = 1.0 / jnp.sum(probs, axis=1, keepdims=True)
            probs = rounded(probs)
            probs_ref[head] = probs
            r.out[rows, at : at + HD] = matmul(probs, value) * inverse
            r.inverse[rows, head : head + 1] = inverse
        for step in range(per_block):
            place = start // tokens + step
            r.att[place] = folded(rounded(r.out[place * tokens : (place + 1) * tokens, :]))
            copy = att_copy(place)

            @pl.when(ctx != place)
            def _():
                copy.start()

    r.att_in[ctx] = r.att[ctx]
    cot_far.wait_recv()
    cot_fwd = wires.send(r.cots.at[2], r.cots.at[3], core)
    wout_far.wait_recv()
    out_at = rows_of(far["dp"])
    wout_fwd = wires.send(r.w_out.at[out_at], r.w_out.at[out_at], core)
    for copy in up_in:
        copy.wait_recv()
    wout_core.wait_recv()
    wout_fwd.wait_recv()
    for copy in (loads.gain_two, loads.bias_two, loads.w_down, loads.b_up):
        copy.wait()
    for step in range(1, ctx_size):
        place = lax.rem(ctx + step, ctx_size)
        arrived(r.att.at[0], r.att_in.at[place], r.att_recv.at[place])
    for place in range(ctx_size):
        r.att_got[place] = unfolded(r.att_in[place])

    gain = r.gain_two[...].reshape(1, model)
    bias = r.bias_two[...].reshape(1, model)
    for at in range(4):

        @pl.when(dp == at)
        def _():
            r.b_own[...] = r.b_up[at * ff : (at + 1) * ff].reshape(1, ff)

    for micro in range(mbs):
        rows = pl.ds(micro * tokens, tokens)
        stream = r.x[rows, :].astype(f32)
        for group in range(groups):
            stream += matmul(
                r.att_got[micro * groups + group], r.w_out[pl.ds(group * width, width), :]
            )
        r.mid[rows, :] = stream
    xhat, inverse_two = norm_parts(r.mid[...])
    r.hat_two[...] = xhat
    r.normed[0] = rounded(xhat * gain + bias)
    to_core = wires.send(r.normed.at[0], r.normed.at[1], core)
    to_far = wires.send(r.normed.at[0], r.normed.at[2], far)

    def feed(slot):
        hidden = matmul(r.normed[slot], r.w_up[...]) + r.b_own[...]
        cdf = 0.5 * (1.0 + lax.erf(hidden * (2.0**-0.5)))
        density = jnp.exp(-0.5 * hidden * hidden) * ((2.0 * math.pi) ** -0.5)
        r.act[slot] = rounded(hidden * cdf)
        grad = contract_cols(r.cots[slot], r.w_down[...])
        r.grad_hid[slot] = rounded(grad * (cdf + hidden * density))
        r.part[slot] = rounded(contract_cols(r.grad_hid[slot], r.w_up[...]))

    def feed_out(slot):
        r.out_part[slot] = rounded(matmul(r.act[slot], r.w_down[...]))

    part_core, part_far_core, forward = (
        wires.later(r.part.at[1], r.part_got.at[0], core),
        wires.later(r.part.at[3], r.part_got.at[1], core),
        wires.later(r.normed.at[2], r.normed.at[3], core),
    )

    def feed_step(slot, carry):
        @pl.when(slot == 1)
        def _():
            cot_core.wait_recv()
            to_core.wait_recv()

        @pl.when(slot == 2)
        def _():
            part_core.start()
            to_far.wait_recv()
            forward.start()

        @pl.when(slot == 3)
        def _():
            forward.wait_recv()
            cot_fwd.wait_recv()

        feed(slot)
        return carry

    lax.fori_loop(0, 4, feed_step, 0)
    part_far_core.start()
    part_far_core.wait_recv()
    r.part[2] = rounded(r.part[2].astype(f32) + r.part_got[1].astype(f32))
    part_far = wires.send(r.part.at[2], r.part_got.at[2], far)
    pair = line // 2
    collects = lax.rem(line, 2) == 1 - pair
    other = pl.ds((1 - pair) * 2, 2)

    def line_copies(at, grad, near, distant, shared):
        def copy(source, target, kind, index, to_line):
            return pltpu.make_async_remote_copy(
                src_ref=source,
                dst_ref=target,
                send_sem=r.line_send.at[at, index],
                recv_sem=r.line_recv.at[at, kind],
                device_id={"ctx": to_line * 2 + side},
                device_id_type=MESH,
            )

        to_near = copy(grad.at[side, swap(line)], near, 0, 0, swap(line))
        to_shared = copy(grad.at[side, other], shared, 1, 1, swap(line))
        to_distant = [
            copy(grad.at[side, (1 - pair) * 2 + step], distant, 2, 1 + step, (1 - pair) * 2 + step)
            for step in range(2)
        ]
        return to_near, to_shared, to_distant

    def line_start(at, side_copy, side_got, grad, *targets):
        side_copy.wait_recv()
        grad[side] = rounded(grad[side].astype(f32) + side_got[...].astype(f32))
        to_near, to_shared, _ = line_copies(at, grad, *targets)
        to_near.start()

        @pl.when(jnp.logical_not(collects))
        def _():
            to_shared.start()

    def line_collect(at, grad, near, distant, shared):
        _, _, to_distant = line_copies(at, grad, near, distant, shared)

        @pl.when(collects)
        def _():
            arrived(grad.at[side, other], shared, r.line_recv.at[at, 1])
            grad[side, other] = rounded(grad[side, other].astype(f32) + shared[...].astype(f32))
            for copy in to_distant:
                copy.start()

    def line_finish(at, grad, near, distant, shared):
        arrived(near, near, r.line_recv.at[at, 0])
        arrived(distant, distant, r.line_recv.at[at, 2])
        return grad[side, line].astype(f32) + near[...].astype(f32) + distant[...].astype(f32)

    def line_drain(at, grad, near, distant, shared):
        to_near, to_shared, to_distant = line_copies(at, grad, near, distant, shared)
        to_near.wait_send()

        @pl.when(jnp.logical_not(collects))
        def _():
            to_shared.wait_send()

        @pl.when(collects)
        def _():
            for copy in to_distant:
                copy.wait_send()

    down_refs = (0, r.down_grad, r.down_near, r.down_distant, r.down_shared)
    up_refs = (1, r.up_grad, r.up_near, r.up_distant, r.up_shared)
    out_refs = (2, r.out_piece, r.out_near, r.out_distant, r.out_shared)

    def start_line(refs, side_copy, side_got):
        line_start(refs[0], side_copy, side_got, *refs[1:])

    flat_cot = r.cots[...].reshape(4 * own, model)
    flat_act = r.act[...].reshape(4 * own, ff)
    grads = rounded(contract_rows(flat_cot, flat_act))
    narrow = model // ctx_size
    for at in range(ctx_size):
        r.down_grad[at % 2, at // 2] = grads[at * narrow : (at + 1) * narrow]
    down_side = wires.send(r.down_grad.at[1 - side], r.down_side, beside)
    out_core, out_far_core = (
        wires.later(r.out_part.at[1], r.out_got.at[0], core),
        wires.later(r.out_part.at[3], r.out_got.at[1], core),
    )

    def out_step(step, carry):
        slot = 3 - step
        feed_out(slot)

        @pl.when(slot == 3)
        def _():
            out_far_core.start()

        @pl.when(slot == 1)
        def _():
            out_core.start()

        return carry

    lax.fori_loop(0, 4, out_step, 0)
    flat_grad = r.grad_hid[...].reshape(4 * own, ff)
    vec_rows = 4 + ff // model
    d_bias_up = jnp.sum(flat_grad.astype(f32), axis=0, keepdims=True)
    for at in range(ff // model):
        r.vec[4 + at : 5 + at, :] = d_bias_up[:, at * model : (at + 1) * model]
    flat_normed = r.normed[...].reshape(4 * own, model)
    size = model // 4
    for at in range(shards):
        grads = rounded(
            contract_rows(flat_normed, flat_grad[:, at * ff // shards : (at + 1) * ff // shards])
        )
        for row in range(4):
            index = at * 4 + row
            r.up_grad[index % 2, index // 2] = grads[row * size : (row + 1) * size]
    out_far_core.wait_recv()
    r.out_part[2] = rounded(r.out_part[2].astype(f32) + r.out_got[1].astype(f32))

    part_core.wait_recv()
    part_far.wait_recv()
    out_far = wires.send(r.out_part.at[2], r.out_got.at[2], far)
    grad_normed = r.part[0].astype(f32) + r.part_got[0].astype(f32) + r.part_got[2].astype(f32)
    xhat = r.hat_two[...]
    r.vec[2:3, :] = jnp.sum(grad_normed * xhat, axis=0, keepdims=True)
    r.vec[3:4, :] = jnp.sum(grad_normed, axis=0, keepdims=True)
    r.grad_mid[...] = r.cot[...].astype(f32) + norm_back(xhat, inverse_two, grad_normed, gain)
    branch = rounded(r.grad_mid[...])
    for group in range(groups):
        grad = rounded(contract_cols(branch, r.w_out[pl.ds(group * width, width), :]))
        for micro in range(mbs):
            r.att_out[micro * groups + group] = folded(
                grad[micro * tokens : (micro + 1) * tokens]
            )
    att_in = []
    for step in range(1, ctx_size):
        peer = lax.rem(ctx + step, ctx_size)
        att_in.append(wires.send(r.att_out.at[peer], r.grad_in.at[ctx], {"ctx": peer}))
    r.grad_in[ctx] = r.att_out[ctx]
    for group in range(groups):
        total = None
        for micro in range(mbs):
            some = contract_rows(
                branch[micro * tokens : (micro + 1) * tokens], r.att_got[micro * groups + group]
            )
            total = some if total is None else total + some
        total = rounded(total)
        for at in range(ctx_size):
            r.out_grad[group, at % 2, at // 2] = folded(total[at * narrow : (at + 1) * narrow])
    out_grad_core = wires.send(r.out_grad.at[swap(dp)], r.out_grad_got.at[0], core)
    out_grad_far_core = wires.send(
        r.out_grad.at[lax.rem(swap(dp) + 2, 4)], r.out_grad_got.at[1], core
    )
    out_grad_far_core.wait_recv()
    mine = lax.rem(dp + 2, 4)
    r.out_grad[mine] = rounded(r.out_grad[mine].astype(f32) + r.out_grad_got[1].astype(f32))
    out_grad_far = wires.send(r.out_grad.at[mine], r.out_grad_got.at[2], far)
    up_side = wires.send(r.up_grad.at[1 - side], r.up_side, beside)
    start_line(down_refs, down_side, r.down_side)
    for copy in att_in:
        copy.wait_recv()
    for place in range(ctx_size):
        r.grad_att[place] = unfolded(r.grad_in[place])

    r.suffix[...] = jnp.zeros_like(r.suffix)
    r.acc[...] = jnp.zeros_like(r.acc)

    def back_block(start):
        reach = start + block
        rows = pl.ds(start, block)
        probs_ref, slope_ref = getattr(r, "probs%d" % start), getattr(r, "slope%d" % start)
        total = None
        first = start // tokens
        grad_block = r.grad_att[first : first + per_block].reshape(block, width)
        for head in range(hpg):
            at = head * HD
            query_t = rounded((r.proj[rows, at : at + HD].astype(f32) * scale).T)
            key = r.proj[:reach, width + at : width + at + HD]
            value = r.proj[:reach, 2 * width + at : 2 * width + at + HD]
            grad = grad_block[:, at : at + HD].astype(f32) * r.inverse[rows, head : head + 1]
            delta = jnp.sum(grad * r.out[rows, at : at + HD], axis=1, keepdims=True)
            probs = probs_ref[head]
            grad_probs = contract_cols(rounded(grad), value)
            grad_logits = probs.astype(f32) * (grad_probs - delta)
            total = grad_logits if total is None else total + grad_logits
            grad_scores = rounded(grad_logits)
            r.grad_proj[rows, at : at + HD] = rounded(matmul(grad_scores, key) * scale)
            r.acc[at : at + HD, :reach] += matmul(query_t, grad_scores)
            r.acc[width + at : width + at + HD, :reach] += matmul(rounded(grad.T), probs)
        query_t = rounded((r.proj[rows, 3 * width : 3 * width + HD].astype(f32) * scale).T)
        key = r.proj[:reach, 3 * width + HD : 3 * width + 2 * HD]
        flow = r.suffix[:, :reach] + matmul(later, rounded(total))
        grad_scores = rounded(-flow * slope_ref[...].astype(f32))
        r.grad_proj[rows, 3 * width : 3 * width + HD] = rounded(matmul(grad_scores, key) * scale)
        r.acc[2 * width : 2 * width + HD, :reach] += matmul(query_t, grad_scores)
        r.suffix[:, :reach] += jnp.sum(total, axis=0, keepdims=True)

    def one_grad(place):
        rows = pl.ds(pl.multiple_of(place * tokens, tokens), tokens)
        grad = contract_cols(r.grad_proj[rows, :], r.w_pick[...].reshape(model, 3 * width + 2 * HD))
        r.vec[0:1, :] += jnp.sum(grad * r.hat_one[rows, :].astype(f32), axis=0, keepdims=True)
        r.vec[1:2, :] += jnp.sum(grad, axis=0, keepdims=True)
        return grad

    r.vec[0:2, :] = jnp.zeros((2, model), f32)
    one_side = {}

    def one_copy(source, target, kind, at, to_line):
        return pltpu.make_async_remote_copy(
            src_ref=source,
            dst_ref=target,
            send_sem=r.one_send.at[at],
            recv_sem=r.one_recv.at[kind],
            device_id={"ctx": to_line * 2 + side},
            device_id_type=MESH,
        )

    def to_near(at):
        return one_copy(r.one_ready.at[at], r.one_near, 0, at, at)

    def to_far(at):
        return one_copy(r.one_ready.at[at], r.one_far, 1, at, at)

    def to_collect(at):
        return one_copy(r.one_ready.at[at], r.one_pair.at[at % 2], 2 + at % 2, at, swap(line))

    def finish_block(at):
        start = at * block
        reach = start + block
        r.grad_proj[start:reach, width : 3 * width] = rounded(r.acc[: 2 * width, start:reach].T)
        r.grad_proj[start:reach, 3 * width + HD :] = rounded(r.acc[2 * width :, start:reach].T)
        one_side[at] = wires.later(r.one_piece.at[at], r.one_side.at[at], beside)

        def one_step(step, carry):
            r.one_own[at] = one_grad(at * 2 + lax.rem(1 - side + step, 2))

            @pl.when(step == 0)
            def _():
                r.one_piece[at] = rounded(r.one_own[at])
                one_side[at].start()

            return carry

        lax.fori_loop(0, 2, one_step, 0)

    def pass_on(at):
        one_side[at].wait_recv()
        r.one_ready[at] = rounded(r.one_own[at] + r.one_side[at].astype(f32))
        near, shared = to_near(at), to_collect(at)

        @pl.when((pair == at // 2) & (line != at))
        def _():
            near.start()

        @pl.when((pair != at // 2) & jnp.logical_not(collects))
        def _():
            shared.start()

    def collect(at):
        distant = to_far(at)

        @pl.when((pair != at // 2) & collects)
        def _():
            arrived(r.one_ready.at[at], r.one_pair.at[at % 2], r.one_recv.at[2 + at % 2])
            r.one_ready[at] = rounded(
                r.one_own[at] + r.one_side[at].astype(f32) + r.one_pair[at % 2].astype(f32)
            )
            distant.start()

    back_block(3 * block)
    finish_block(3)
    back_block(2 * block)
    finish_block(2)
    line_collect(*down_refs)
    start_line(up_refs, up_side, r.up_side)
    back_block(block)
    finish_block(1)
    pass_on(3)
    back_block(0)
    finish_block(0)
    vec_in = []
    for step in range(1, ctx_size):
        peer = lax.rem(ctx + step, ctx_size)
        vec_in.append(wires.send(r.vec, r.vec_got.at[ctx], {"ctx": peer}))
    r.vec_got[ctx] = r.vec[...]
    out_grad_core.wait_recv()
    out_grad_far.wait_recv()
    r.out_piece[...] = rounded(
        r.out_grad[dp].astype(f32)
        + r.out_grad_got[0].astype(f32)
        + r.out_grad_got[2].astype(f32)
    )
    out_side = wires.send(r.out_piece.at[1 - side], r.out_side, beside)

    size = model // 4
    part = math.gcd(width, 3 * model // ctx_size)
    per = width // part
    folded_part, folded_head = part // 2, HD // 2

    def store_qkv(grads, parts):
        for at in range(4):
            cols = slice(at * size, (at + 1) * size)
            for source, target, count in parts:
                r.qkv_grad[at, target : target + count // 2, :] = folded(
                    grads[source : source + count, cols]
                )

    tail = 3 * width // 2
    grads_q = rounded(
        contract_rows(
            jnp.concatenate(
                [r.grad_proj[:, :width], r.grad_proj[:, 3 * width : 3 * width + HD]], axis=1
            ),
            r.normed_one[...],
        )
    )
    store_qkv(
        grads_q,
        [(at * part, at * folded_part, part) for at in range(per)] + [(width, tail, HD)],
    )
    pass_on(2)
    grads_kv = rounded(matmul(rounded(r.acc[...]), r.normed_one[...]))
    store_qkv(
        grads_kv,
        [(at * part, (per + at) * folded_part, part) for at in range(2 * per)]
        + [(2 * width, tail + folded_head, HD)],
    )
    qkv_far_core = wires.send(r.qkv_grad.at[lax.rem(swap(dp) + 2, 4)], r.qkv_got.at[1], core)
    qkv_core = wires.send(r.qkv_grad.at[swap(dp)], r.qkv_got.at[0], core)
    collect(3)
    line_collect(*up_refs)
    pass_on(1)
    qkv_far_core.wait_recv()
    r.qkv_grad[mine] = rounded(r.qkv_grad[mine].astype(f32) + r.qkv_got[1].astype(f32))
    qkv_far = wires.send(r.qkv_grad.at[mine], r.qkv_got.at[2], far)
    collect(2)
    pass_on(0)
    collect(1)
    start_line(out_refs, out_side, r.out_side)
    collect(0)
    line_collect(*out_refs)
    r.d_down[...] = line_finish(*down_refs)
    out_core.wait_recv()
    out_far.wait_recv()
    r.layer[...] = rounded(
        r.mid[...]
        + (r.out_part[0].astype(f32) + r.out_got[0].astype(f32) + r.out_got[2].astype(f32))
    )
    r.up_sum[...] = rounded(line_finish(*up_refs))
    stays = (lax.rem(ctx, 4) == dp) & (shards * dp + ctx // 4 == ctx)
    up_copy = pltpu.make_async_remote_copy(
        src_ref=r.up_sum,
        dst_ref=r.up_final,
        send_sem=r.up_send.at[0],
        recv_sem=r.up_recv.at[0],
        device_id=up_to,
        device_id_type=MESH,
    )

    @pl.when(jnp.logical_not(stays))
    def _():
        up_copy.start()

    @pl.when(stays)
    def _():
        r.up_final[...] = r.up_sum[...]

    for copy in vec_in:
        copy.wait_recv()
    total = r.vec_got[0]
    for at in range(1, ctx_size):
        total += r.vec_got[at]
    r.vec_sum[...] = total
    vec_out = [
        wires.send(r.vec_sum, r.vecs.at[dp], where) for where in (core, far, far_core)
    ]
    r.vecs[dp] = total
    qkv_core.wait_recv()
    qkv_far.wait_recv()
    r.qkv_sum[...] = rounded(
        r.qkv_grad[dp].astype(f32) + r.qkv_got[0].astype(f32) + r.qkv_got[2].astype(f32)
    )
    slots = r.deal_got.shape[0]

    def outgoing(kind, half):
        section = (kind * groups + my_group) * per + half
        target, slot = section // slots, lax.rem(section, slots)
        index = kind * per + half
        return target, slot, index, pltpu.make_async_remote_copy(
            src_ref=r.qkv_sum.at[pl.ds(index * folded_part, folded_part)],
            dst_ref=r.deal_got.at[slot, my_mb],
            send_sem=r.deal_send.at[index],
            recv_sem=r.deal_recv.at[slot, my_mb],
            device_id={"ctx": target},
            device_id_type=MESH,
        )

    def extra_copy(kind):
        return pltpu.make_async_remote_copy(
            src_ref=r.qkv_sum.at[pl.ds(tail + kind * folded_head, folded_head)],
            dst_ref=r.extra_got.at[ctx],
            send_sem=r.extra_send.at[kind],
            recv_sem=r.extra_recv.at[ctx],
            device_id={"ctx": kind * groups * per // slots},
            device_id_type=MESH,
        )

    for kind in range(3):
        for half in range(per):
            target, slot, index, copy = outgoing(kind, half)

            @pl.when(target != ctx)
            def _():
                copy.start()

            @pl.when(target == ctx)
            def _():
                r.deal_got[slot, my_mb] = r.qkv_sum[
                    index * folded_part : (index + 1) * folded_part, :
                ]

    for kind in range(2):
        target = kind * groups * per // slots
        copy = extra_copy(kind)

        @pl.when(ctx != target)
        def _():
            copy.start()

        @pl.when(ctx == target)
        def _():
            r.extra_got[ctx] = r.qkv_sum[
                tail + kind * folded_head : tail + (kind + 1) * folded_head, :
            ]

    xhat, inverse_one = norm_parts(r.x[...].astype(f32))
    arrived(r.one_ready.at[0], r.one_near, r.one_recv.at[0])
    arrived(r.one_ready.at[0], r.one_far, r.one_recv.at[1])
    near = r.one_ready[line].astype(f32) + r.one_near[...].astype(f32)
    distant = r.one_far[...].astype(f32)
    for micro in range(mbs):
        grad = jnp.where(pair == micro, near, distant)
        rows = slice(micro * tokens, (micro + 1) * tokens)
        r.d_x[rows, :] = rounded(
            r.grad_mid[rows, :] + norm_back(xhat[rows], inverse_one[rows], grad, gain_one)
        )
    r.d_out[...] = unfolded(line_finish(*out_refs)).T

    @pl.when(jnp.logical_not(stays))
    def _():
        up_copy.wait_send()
        up_copy.wait_recv()

    r.d_up[...] = r.up_final[...].astype(f32)

    for kind in range(3):
        for half in range(per):
            target, slot, index, copy = outgoing(kind, half)

            @pl.when(target != ctx)
            def _():
                copy.wait_send()

    for slot in range(slots):
        section = ctx * slots + slot
        source_group = lax.rem(section // per, groups)
        for place in range(mbs):

            @pl.when(place * groups + source_group != ctx)
            def _():
                arrived(
                    r.qkv_sum.at[pl.ds(0, folded_part)],
                    r.deal_got.at[slot, place],
                    r.deal_recv.at[slot, place],
                )

        total = r.deal_got[slot, 0].astype(f32)
        for place in range(1, mbs):
            total += r.deal_got[slot, place].astype(f32)
        r.deal_sum[slot * part : (slot + 1) * part, :] = unfolded(total)
    for kind in range(2):
        section = kind * groups * per
        target, slot = section // slots, section % slots
        copy = extra_copy(kind)

        @pl.when(ctx != target)
        def _():
            copy.wait_send()

        @pl.when(ctx == target)
        def _():
            total = jnp.zeros((folded_head, 2 * size), f32)
            for place in range(ctx_size):
                if place != target:
                    arrived(
                        r.qkv_sum.at[pl.ds(0, folded_head)], r.extra_got.at[place], r.extra_recv.at[place]
                    )
                total += r.extra_got[place].astype(f32)
            r.deal_sum[slot * part : slot * part + HD, :] += unfolded(total)

    r.d_qkv[...] = r.deal_sum[...].T
    for copy in vec_out:
        copy.wait_recv()
    for row in range(4):
        r.d_vec[row : row + 1, :] = (
            r.vecs[0, row : row + 1, :] + r.vecs[1, row : row + 1, :]
        ) + (r.vecs[2, row : row + 1, :] + r.vecs[3, row : row + 1, :])
    for at in range(4):
        r.d_bias[at] = r.vecs[at, 4:vec_rows, :]
    wires.drain()
    for refs in (down_refs, up_refs, out_refs):
        line_drain(*refs)
    for place in range(ctx_size):
        copy = att_copy(place)

        @pl.when(ctx != place)
        def _():
            copy.wait_send()

    for at in range(lines):
        copy = to_near(at)

        @pl.when(line != at)
        def _():
            copy.wait_send()


LAYER_COPIES = 96


def layer(collective_id, groups, shards, lengths, large):
    bf16, f32 = jnp.bfloat16, jnp.float32
    own, model = large["x"].shape
    ctx_size = lax.axis_size("ctx")
    tokens = own * groups // ctx_size
    hpg = model // HD // groups
    width = hpg * HD
    row_length = ctx_size * tokens
    lines = ctx_size // 2
    ff = large["w_down"].shape[0]
    size, shard = model // 4, 3 * model // ctx_size
    part = math.gcd(width, shard)
    slots, mbs = shard // part, ctx_size // groups
    picked = 3 * width + 2 * HD
    vec_rows = 4 + ff // model
    narrow = model // ctx_size
    vmem = pl.BlockSpec(memory_space=pltpu.VMEM)
    anywhere = pl.BlockSpec(memory_space=pl.ANY)
    outs = dict(
        layer=((own, model), bf16),
        d_x=((own, model), bf16),
        d_vec=((4, model), f32),
        d_bias=((4, ff // model, model), f32),
        d_qkv=((size, shard), f32),
        d_out=((size, narrow), f32),
        d_up=((size, ff // shards), f32),
        d_down=((narrow, ff), f32),
    )
    scratch = {name: (array.shape, array.dtype) for name, array in large.items()}
    scratch |= dict(
        x_row=((ctx_size, tokens, model), bf16),
        hat_one=((row_length, model), bf16),
        normed_one=((row_length, model), bf16),
        w_pick=((4, size, picked), bf16),
        proj=((row_length, picked), bf16),
        w_out=((model, model), bf16),
        w_up=((model, ff), bf16),
        out=((row_length, width), f32),
        inverse=((row_length, hpg), f32),
        att=((ctx_size, tokens // 2, 2 * width), bf16),
        att_in=((ctx_size, tokens // 2, 2 * width), bf16),
        b_own=((1, ff), f32),
        att_got=((ctx_size, tokens, width), bf16),
        cots=((4, own, model), bf16),
        mid=((own, model), f32),
        hat_two=((own, model), f32),
        grad_mid=((own, model), f32),
        normed=((4, own, model), bf16),
        act=((4, own, ff), bf16),
        grad_hid=((4, own, ff), bf16),
        part=((4, own, model), bf16),
        out_part=((4, own, model), bf16),
        part_got=((3, own, model), bf16),
        out_got=((3, own, model), bf16),
        att_out=((ctx_size, tokens // 2, 2 * width), bf16),
        grad_in=((ctx_size, tokens // 2, 2 * width), bf16),
        grad_att=((ctx_size, tokens, width), bf16),
        down_grad=((2, lines, narrow, ff), bf16),
        down_side=((lines, narrow, ff), bf16),
        down_near=((narrow, ff), bf16),
        down_distant=((narrow, ff), bf16),
        down_shared=((2, narrow, ff), bf16),
        up_grad=((2, lines, size, ff // shards), bf16),
        up_side=((lines, size, ff // shards), bf16),
        up_near=((size, ff // shards), bf16),
        up_distant=((size, ff // shards), bf16),
        up_shared=((2, size, ff // shards), bf16),
        up_sum=((size, ff // shards), bf16),
        up_final=((size, ff // shards), bf16),
        out_grad=((4, 2, lines, narrow // 2, 2 * size), bf16),
        out_grad_got=((3, 2, lines, narrow // 2, 2 * size), bf16),
        out_piece=((2, lines, narrow // 2, 2 * size), bf16),
        out_side=((lines, narrow // 2, 2 * size), bf16),
        out_near=((narrow // 2, 2 * size), bf16),
        out_distant=((narrow // 2, 2 * size), bf16),
        out_shared=((2, narrow // 2, 2 * size), bf16),
        suffix=((1, row_length), f32),
        acc=((2 * width + HD, row_length), f32),
        grad_proj=((row_length, picked), bf16),
        one_piece=((lines, tokens, model), bf16),
        one_own=((lines, tokens, model), f32),
        one_side=((lines, tokens, model), bf16),
        one_ready=((lines, tokens, model), bf16),
        one_near=((tokens, model), bf16),
        one_far=((tokens, model), bf16),
        one_pair=((2, tokens, model), bf16),
        qkv_grad=((4, picked // 2, 2 * size), bf16),
        qkv_got=((3, picked // 2, 2 * size), bf16),
        qkv_sum=((picked // 2, 2 * size), bf16),
        deal_got=((slots, mbs, part // 2, 2 * size), bf16),
        deal_sum=((shard, size), f32),
        extra_got=((ctx_size, HD // 2, 2 * size), bf16),
        vec=((vec_rows, model), f32),
        vec_got=((ctx_size, vec_rows, model), f32),
        vec_sum=((vec_rows, model), f32),
        vecs=((4, vec_rows, model), f32),
    )
    for start in range(0, row_length, QUERY_BLOCK):
        reach = start + QUERY_BLOCK
        scratch["probs%d" % start] = ((hpg, QUERY_BLOCK, reach), bf16)
        scratch["slope%d" % start] = ((QUERY_BLOCK, reach), bf16)
    dma = pltpu.SemaphoreType.DMA
    sems = dict(
        send_sem=dma((LAYER_COPIES,)),
        recv_sem=dma((LAYER_COPIES,)),
        load_sem=dma((len(large),)),
        att_send=dma((ctx_size,)),
        att_recv=dma((ctx_size,)),
        one_send=dma((lines,)),
        one_recv=dma((4,)),
        line_send=dma((3, 3)),
        line_recv=dma((3, 3)),
        up_send=dma((1,)),
        up_recv=dma((1,)),
        deal_send=dma((3 * (width // part),)),
        deal_recv=dma((slots, mbs)),
        extra_send=dma((2,)),
        extra_recv=dma((ctx_size,)),
    )
    names = list(outs) + list(scratch) + list(sems)
    return pl.pallas_call(
        partial(layer_body, (groups, shards), list(large), names),
        out_shape=[jax.ShapeDtypeStruct(*spec) for spec in outs.values()],
        in_specs=[pl.BlockSpec(memory_space=pltpu.SMEM)] + [anywhere] * len(large),
        out_specs=[vmem] * len(outs),
        scratch_shapes=[pltpu.VMEM(*spec) for spec in scratch.values()] + list(sems.values()),
        compiler_params=pltpu.CompilerParams(
            collective_id=collective_id, has_side_effects=True, vmem_limit_bytes=63 * 1024 * 1024
        ),
        name="layer",
    )(lengths, *large.values())


def finish_body(*refs):
    sources, targets = refs[:8], refs[8:]
    for source, target in zip(sources[:6], targets[:6]):
        target[...] = source[...]
    for row in range(4):
        targets[6 + row][...] = sources[6][row]
    columns = sources[7].shape[2]
    rows = sources[7].shape[1]
    for at in range(4 * rows):
        targets[10][at * columns : (at + 1) * columns] = sources[7][at // rows, at % rows]


def finish(*arrays):
    vmem = pl.BlockSpec(memory_space=pltpu.VMEM)
    shape = jax.ShapeDtypeStruct
    model = arrays[6].shape[1]
    return pl.pallas_call(
        finish_body,
        out_shape=[shape(array.shape, array.dtype) for array in arrays[:6]]
        + [shape((model,), jnp.float32)] * 4
        + [shape((arrays[7].size,), jnp.float32)],
        in_specs=[vmem] * len(arrays),
        out_specs=[vmem] * 11,
        name="finish",
    )(*arrays)


def per_head_device(
    layer_input,
    doc_lengths,
    ln1_gain,
    ln1_bias,
    w_qkv,
    w_out,
    ln2_gain,
    ln2_bias,
    w_up,
    b_up,
    w_down,
    cotangent,
):
    mbs, _, tokens, model = layer_input.shape
    ctx_size, dp_size = lax.axis_size("ctx"), lax.axis_size("dp")
    large = dict(
        x=layer_input.reshape(mbs * tokens, model),
        w_qkv=w_qkv,
        gain_one=ln1_gain,
        bias_one=ln1_bias,
        cot=cotangent.reshape(mbs * tokens, model),
        w_out_own=w_out,
        w_up_own=w_up,
        gain_two=ln2_gain,
        bias_two=ln2_bias,
        w_down=w_down,
        b_up=b_up,
    )
    layer_out, d_x, d_vec, d_bias, d_qkv, d_out, d_up, d_down = layer(
        0, ctx_size // mbs, ctx_size // dp_size, doc_lengths, large
    )
    layer_out, d_x, d_qkv, d_out, d_up, d_down, gain_one, bias_one, gain_two, bias_two, d_bias = finish(
        layer_out, d_x, d_qkv, d_out, d_up, d_down, d_vec, d_bias
    )
    return (
        layer_out.reshape(mbs, 1, tokens, model),
        d_x.reshape(mbs, 1, tokens, model),
        gain_one,
        bias_one,
        d_qkv,
        d_out,
        gain_two,
        bias_two,
        d_up,
        d_bias,
        d_down.T,
    )


def on_device(*arguments):
    layer_input = arguments[0]
    mbs, model = layer_input.shape[0], layer_input.shape[3]
    heads, ctx_size, dp_size = model // HD, lax.axis_size("ctx"), lax.axis_size("dp")
    groups = ctx_size // mbs
    fits = (
        ctx_size % mbs == 0
        and heads % groups == 0
        and dp_size == 4
        and ctx_size % dp_size == 0
        and ctx_size == 8
        and mbs == 2
        and (layer_input.shape[2] * ctx_size) % QUERY_BLOCK == 0
    )
    return (per_head_device if fits else per_token_device)(*arguments)


def solution(mesh):
    return jax.shard_map(
        on_device,
        mesh=mesh,
        in_specs=(
            P(None, "dp", "ctx", None),
            P(None, "dp", None),
            P(),
            P(),
            P("dp", None),
            P("dp", None),
            P(),
            P(),
            P("dp", None),
            P(),
            P("dp", None),
            P(None, "dp", "ctx", None),
        ),
        out_specs=(
            P(None, "dp", "ctx", None),
            P(None, "dp", "ctx", None),
            P(),
            P(),
            P("dp", "ctx"),
            P("dp", "ctx"),
            P(),
            P(),
            P("dp", "ctx"),
            P(),
            P("dp", "ctx"),
        ),
        check_vma=False,
    )
```

profile of v0, /device:TPU:0, one launch (start us, length us, event | category | flops | bytes accessed | tf_op | source)
XLA Modules:
  0.0 150.1 jit_solution(3770904991917218408)
XLA Ops:
  0.6 146.5 %layer.1 = (bf16[256,768]{1,0:T(8,128)(2,1)}, bf16[256,768]{1,0:T(8,128)(2,1)}, f32[4,768]{1,0:T(4,128)}, f32[4,1,768]{2,1,0:T(1,128)}, f32[192,288]{1,0:T(8,128...) custom-call(s32[2,1,5]{2,1,0:T(1,128)} %lengths.1, bf16[256,768]{1,0:T(8,128)(2,1)} %bitcast.9, ...), custom_call_target="tpu_custom_call" | custom-call | tf_op jit(solution)/shard_map/layer/pallas_call | solution.py:1379
  147.2 2.7 %finish.1 = (bf16[256,768]{1,0:T(8,128)(2,1)}, bf16[256,768]{1,0:T(8,128)(2,1)}, f32[192,288]{1,0:T(8,128)}, f32[192,96]{1,0:T(8,128)}, f32[192,384]{1,0:T(8,128...) custom-call(bf16[256,768]{1,0:T(8,128)(2,1)} %get-tuple-element.30.r, ...), custom_call_target="tpu_custom_call" | custom-call | tf_op jit(solution)/shard_map/finish/pallas_call | solution.py:1408
where the time goes:
time: 150 us
  Pallas kernels  149 us (99%)
    pallas_call x1, Pallas kernels, layer(): pl.pallas_call(partial(layer_body, (groups, shards), list(large), names),...  147 us

commit v1 on v0

--- a/solution.py
+++ b/solution.py
@@ -415,6 +415,10 @@
         self.made.append(copy)
         return copy
 
+    def sent(self, copy):
+        copy.wait_send()
+        self.made.remove(copy)
+
     def drain(self):
         for copy in self.made:
             copy.wait_send()
@@ -442,7 +446,7 @@
     return index + 1 - 2 * lax.rem(index, 2)
 
 
-def layer_body(plan, loaded, names, lengths, *refs):
+def layer_body(plan, loaded, names, lengths, w_down, *refs):
     given, refs = refs[: len(loaded)], refs[len(loaded) :]
     r = SimpleNamespace(**dict(zip(names, refs)))
     groups, shards = plan
@@ -454,15 +458,20 @@
     mbs = ctx_size // groups
     hpg = width // HD
     own = r.x.shape[0]
-    ff = r.w_down.shape[0]
+    ff = r.w_ff.shape[0]
     row_length = tokens * ctx_size
     side, line = lax.rem(ctx, 2), ctx // 2
     my_mb, my_group = ctx // groups, lax.rem(ctx, groups)
     wires = Wires(r.send_sem, r.recv_sem)
     core, far, far_core = {"dp": swap(dp)}, {"dp": lax.rem(dp + 2, 4)}, {"dp": lax.rem(swap(dp) + 2, 4)}
     beside = {"ctx": swap(ctx)}
-    up_to = {"dp": lax.rem(ctx, 4), "ctx": shards * dp + ctx // 4}
-    up_from = {"dp": ctx // shards, "ctx": lax.rem(ctx, shards) * 4 + dp}
+    upper, which = dp // 2, lax.rem(dp, 2)
+    odd, distant_half = lax.rem(line, 2), line // 2
+    ff_block = 2 * odd + which
+    owns_block = ff_block == dp
+    up_to = {"dp": 2 * upper + distant_half, "ctx": 2 * ff_block + side}
+    up_from = {"dp": 2 * upper + lax.rem(line, 2), "ctx": 2 * (2 * which + line // 2) + side}
+    across = {"dp": ff_block, "ctx": 2 * (2 * distant_half + upper) + side}
     around = [{"ctx": lax.rem(ctx + step, ctx_size)} for step in range(1, ctx_size)]
 
     mirror = {"ctx": lax.rem(line + lines // 2, lines) * 2 + side}
@@ -475,19 +484,34 @@
         copy = pltpu.make_async_copy(given[at], getattr(r, name), r.load_sem.at[at])
         copy.start()
         setattr(loads, name, copy)
+    down_load = pltpu.make_async_copy(w_down, r.w_ff, r.ff_sem.at[0])
+    down_copy = pltpu.make_async_remote_copy(
+        src_ref=w_down,
+        dst_ref=r.w_ff,
+        send_sem=r.ff_sem.at[1],
+        recv_sem=r.ff_sem.at[2],
+        device_id=far,
+        device_id_type=MESH,
+    )
+    pl.when(owns_block)(down_load.start)
     barrier = pltpu.get_barrier_semaphore()
-    for where in around + [core, far, far_core, up_from]:
+    for where in around + [core, far, far_core, up_from, across]:
         pl.semaphore_signal(barrier, inc=1, device_id=where, device_id_type=MESH)
     loads.x.wait()
     loads.w_qkv.wait()
-    pl.semaphore_wait(barrier, ctx_size + 3)
+    pl.semaphore_wait(barrier, ctx_size + 4)
 
     def x_of(micro):
         return r.x.at[pl.ds(pl.multiple_of(micro * tokens, tokens), tokens)]
 
-    x_mirror = wires.send(x_of(1 - my_mb), r.x_row.at[ctx], mirror)
+    first, second = pl.ds(0, tokens // 2), pl.ds(tokens // 2, tokens // 2)
+
+    def x_half(micro, at):
+        rows = pl.ds(pl.multiple_of(micro * tokens + at * (tokens // 2), tokens // 2), tokens // 2)
+        return r.x.at[rows]
+
+    x_mirror_a = wires.send(x_half(1 - my_mb, 0), r.x_row.at[ctx, first], mirror)
     x_beside = wires.send(x_of(my_mb), r.x_row.at[ctx], beside)
-    x_ahead = wires.send(x_of(my_mb), r.x_row.at[ctx], ahead)
     for group in range(groups):
 
         @pl.when(my_group == group)
@@ -515,14 +539,13 @@
     wout_core = wires.send(r.w_out_own, r.w_out.at[rows_of(dp)], core)
 
     def up_part(peer):
-        return r.w_up_own.at[:, pl.ds(pl.multiple_of(peer * ff, 128), ff)]
+        block = 2 * odd + lax.rem(peer, 2)
+        return r.w_up_own.at[:, pl.ds(pl.multiple_of(block * ff, 128), ff)]
 
     up_in = [
         wires.send(up_part(where["dp"]), r.w_up.at[rows_of(dp)], where)
         for where in (far, far_core, core)
     ]
-    cot_far = wires.send(r.cot, r.cots.at[2], far)
-    cot_core = wires.send(r.cot, r.cots.at[1], core)
     r.w_out[rows_of(dp), :] = r.w_out_own[...]
     r.w_up[rows_of(dp), :] = up_part(dp)[...]
     r.cots[0] = r.cot[...]
@@ -538,38 +561,51 @@
         r.hat_one[rows, :] = rounded(xhat)
         r.normed_one[rows, :] = rounded(xhat * gain_one + bias_one)
 
+    wires.sent(x_mirror_a)
+    x_mirror_b = wires.send(x_half(1 - my_mb, 1), r.x_row.at[ctx, second], mirror)
+    x_ahead = wires.send(x_of(my_mb), r.x_row.at[ctx], ahead)
+    normalise(ctx)
+    mirror_beside, mirror_ahead = swap(mirror_at), lax.rem(ahead_at + ctx_size // 2, ctx_size)
+
+    def relay(place, part, where):
+        return wires.send(r.x_row.at[place, part], r.x_row.at[place, part], where)
+
+    x_mirror_a.wait_recv()
+    a_beside = relay(mirror_at, first, beside)
+    a_ahead = relay(mirror_at, first, ahead)
     x_beside.wait_recv()
     top, bottom = pl.ds(0, half), pl.ds(half, tokens - half)
-    x_fwd_a = wires.send(r.x_row.at[beside_at, top], r.x_row.at[beside_at, top], ahead)
+    x_fwd_a = relay(beside_at, top, ahead)
+    normalise(beside_at)
+    x_mirror_b.wait_recv()
+    b_beside = relay(mirror_at, second, beside)
+    b_ahead = relay(mirror_at, second, ahead)
     x_ahead.wait_recv()
-    x_fwd_b = wires.send(r.x_row.at[ahead_at, bottom], r.x_row.at[ahead_at, bottom], beside)
-    normalise(ctx)
-    x_mirror.wait_recv()
-    x_mirror_beside = wires.send(r.x_row.at[mirror_at], r.x_row.at[mirror_at], beside)
-    x_mirror_ahead = wires.send(r.x_row.at[mirror_at], r.x_row.at[mirror_at], ahead)
+    x_fwd_b = relay(ahead_at, bottom, beside)
+    a_beside.wait_recv()
+    a_over = relay(mirror_beside, first, ahead)
+    pl.when(owns_block)(down_copy.start)
     pick_far.wait_recv()
     pick_at = far["dp"]
     pick_fwd = wires.send(r.w_pick.at[pick_at], r.w_pick.at[pick_at], core)
-
-    normalise(beside_at)
     normalise(ahead_at)
     normalise(mirror_at)
-    x_mirror_beside.wait_recv()
-    place = swap(mirror_at)
-    x_fwd_c = wires.send(r.x_row.at[place, top], r.x_row.at[place, top], ahead)
-    x_mirror_ahead.wait_recv()
-    place = lax.rem(ahead_at + ctx_size // 2, ctx_size)
-    x_fwd_d = wires.send(r.x_row.at[place, bottom], r.x_row.at[place, bottom], beside)
-    normalise(swap(mirror_at))
-    normalise(place)
+    b_ahead.wait_recv()
+    b_over = relay(mirror_ahead, second, beside)
+    a_ahead.wait_recv()
+    b_beside.wait_recv()
+    normalise(mirror_beside)
+    normalise(mirror_ahead)
     x_fwd_a.wait_recv()
     x_fwd_b.wait_recv()
     normalise(swap(ahead_at))
     pick_core.wait_recv()
     pick_fwd.wait_recv()
-    x_fwd_c.wait_recv()
-    x_fwd_d.wait_recv()
-    normalise(swap(place))
+    a_over.wait_recv()
+    b_over.wait_recv()
+    normalise(swap(mirror_ahead))
+    cot_far = wires.send(r.cot, r.cots.at[2], ahead)
+    cot_core = wires.send(r.cot, r.cots.at[1], core)
     w_pick = r.w_pick[...].reshape(model, 3 * width + 2 * HD)
     r.proj[...] = rounded(matmul(r.normed_one[...], w_pick))
 
@@ -617,7 +653,7 @@
         scores = contract_cols(query, key)
         small = jnp.exp(-jnp.abs(scores))
         soft = jnp.maximum(scores, 0.0) + jnp.log(1.0 + small)
-        recip = 1.0 / (1.0 + small)
+        recip = pl.reciprocal(1.0 + small, approx=True)
         sigmoid = jnp.where(scores >= 0.0, recip, small * recip)
         chosen = (row_seg == pick_seg) & (col_pos < row_pos)
         picked = jnp.where(chosen, strength * soft, 0.0)
@@ -660,7 +696,7 @@
         copy.wait_recv()
     wout_core.wait_recv()
     wout_fwd.wait_recv()
-    for copy in (loads.gain_two, loads.bias_two, loads.w_down, loads.b_up):
+    for copy in (loads.gain_two, loads.bias_two, loads.b_up):
         copy.wait()
     for step in range(1, ctx_size):
         place = lax.rem(ctx + step, ctx_size)
@@ -672,7 +708,7 @@
     bias = r.bias_two[...].reshape(1, model)
     for at in range(4):
 
-        @pl.when(dp == at)
+        @pl.when(ff_block == at)
         def _():
             r.b_own[...] = r.b_up[at * ff : (at + 1) * ff].reshape(1, ff)
 
@@ -688,126 +724,111 @@
     r.hat_two[...] = xhat
     r.normed[0] = rounded(xhat * gain + bias)
     to_core = wires.send(r.normed.at[0], r.normed.at[1], core)
-    to_far = wires.send(r.normed.at[0], r.normed.at[2], far)
+    to_far = wires.send(r.normed.at[0], r.normed.at[2], ahead)
 
     def feed(slot):
         hidden = matmul(r.normed[slot], r.w_up[...]) + r.b_own[...]
         cdf = 0.5 * (1.0 + lax.erf(hidden * (2.0**-0.5)))
         density = jnp.exp(-0.5 * hidden * hidden) * ((2.0 * math.pi) ** -0.5)
         r.act[slot] = rounded(hidden * cdf)
-        grad = contract_cols(r.cots[slot], r.w_down[...])
-        r.grad_hid[slot] = rounded(grad * (cdf + hidden * density))
+        r.part[slot] = rounded(cdf + hidden * density)
+
+    def feed_back(slot):
+        grad = contract_cols(r.cots[slot], r.w_ff[...])
+        r.grad_hid[slot] = rounded(grad * r.part[slot].astype(f32))
         r.part[slot] = rounded(contract_cols(r.grad_hid[slot], r.w_up[...]))
 
     def feed_out(slot):
-        r.out_part[slot] = rounded(matmul(r.act[slot], r.w_down[...]))
-
-    part_core, part_far_core, forward = (
+        r.out_part[slot] = rounded(matmul(r.act[slot], r.w_ff[...]))
+
+    part_core, part_far_core, part_far, forward = (
         wires.later(r.part.at[1], r.part_got.at[0], core),
         wires.later(r.part.at[3], r.part_got.at[1], core),
+        wires.later(r.part.at[2], r.part_got.at[2], ahead),
         wires.later(r.normed.at[2], r.normed.at[3], core),
     )
 
     def feed_step(slot, carry):
         @pl.when(slot == 1)
         def _():
-            cot_core.wait_recv()
             to_core.wait_recv()
 
         @pl.when(slot == 2)
         def _():
-            part_core.start()
             to_far.wait_recv()
             forward.start()
 
         @pl.when(slot == 3)
         def _():
             forward.wait_recv()
-            cot_fwd.wait_recv()
 
         feed(slot)
         return carry
 
     lax.fori_loop(0, 4, feed_step, 0)
-    part_far_core.start()
-    part_far_core.wait_recv()
-    r.part[2] = rounded(r.part[2].astype(f32) + r.part_got[1].astype(f32))
-    part_far = wires.send(r.part.at[2], r.part_got.at[2], far)
+    cot_core.wait_recv()
+    cot_fwd.wait_recv()
+    pl.when(owns_block)(down_load.wait)
+    pl.when(jnp.logical_not(owns_block))(down_copy.wait_recv)
+
+    def feed_back_step(step, carry):
+        slot = 3 - step
+        feed_back(slot)
+
+        @pl.when(slot == 3)
+        def _():
+            part_far_core.start()
+
+        @pl.when(slot == 2)
+        def _():
+            part_far_core.wait_recv()
+            r.part[2] = rounded(r.part[2].astype(f32) + r.part_got[1].astype(f32))
+            part_far.start()
+
+        @pl.when(slot == 1)
+        def _():
+            part_core.start()
+
+        return carry
+
+    lax.fori_loop(0, 4, feed_back_step, 0)
     pair = line // 2
     collects = lax.rem(line, 2) == 1 - pair
-    other = pl.ds((1 - pair) * 2, 2)
-
-    def line_copies(at, grad, near, distant, shared):
-        def copy(source, target, kind, index, to_line):
-            return pltpu.make_async_remote_copy(
-                src_ref=source,
-                dst_ref=target,
-                send_sem=r.line_send.at[at, index],
-                recv_sem=r.line_recv.at[at, kind],
-                device_id={"ctx": to_line * 2 + side},
-                device_id_type=MESH,
-            )
-
-        to_near = copy(grad.at[side, swap(line)], near, 0, 0, swap(line))
-        to_shared = copy(grad.at[side, other], shared, 1, 1, swap(line))
-        to_distant = [
-            copy(grad.at[side, (1 - pair) * 2 + step], distant, 2, 1 + step, (1 - pair) * 2 + step)
-            for step in range(2)
-        ]
-        return to_near, to_shared, to_distant
-
-    def line_start(at, side_copy, side_got, grad, *targets):
-        side_copy.wait_recv()
-        grad[side] = rounded(grad[side].astype(f32) + side_got[...].astype(f32))
-        to_near, to_shared, _ = line_copies(at, grad, *targets)
-        to_near.start()
-
-        @pl.when(jnp.logical_not(collects))
-        def _():
-            to_shared.start()
-
-    def line_collect(at, grad, near, distant, shared):
-        _, _, to_distant = line_copies(at, grad, near, distant, shared)
-
-        @pl.when(collects)
-        def _():
-            arrived(grad.at[side, other], shared, r.line_recv.at[at, 1])
-            grad[side, other] = rounded(grad[side, other].astype(f32) + shared[...].astype(f32))
-            for copy in to_distant:
-                copy.start()
-
-    def line_finish(at, grad, near, distant, shared):
-        arrived(near, near, r.line_recv.at[at, 0])
-        arrived(distant, distant, r.line_recv.at[at, 2])
-        return grad[side, line].astype(f32) + near[...].astype(f32) + distant[...].astype(f32)
-
-    def line_drain(at, grad, near, distant, shared):
-        to_near, to_shared, to_distant = line_copies(at, grad, near, distant, shared)
-        to_near.wait_send()
-
-        @pl.when(jnp.logical_not(collects))
-        def _():
-            to_shared.wait_send()
-
-        @pl.when(collects)
-        def _():
-            for copy in to_distant:
-                copy.wait_send()
-
-    down_refs = (0, r.down_grad, r.down_near, r.down_distant, r.down_shared)
-    up_refs = (1, r.up_grad, r.up_near, r.up_distant, r.up_shared)
-    out_refs = (2, r.out_piece, r.out_near, r.out_distant, r.out_shared)
-
-    def start_line(refs, side_copy, side_got):
-        line_start(refs[0], side_copy, side_got, *refs[1:])
+    mirrored = {"ctx": mirror_at}
+    down_steps = (r.down_grad, (upper, side, distant_half), (far, beside, mirrored), (r.down_y, r.down_x, r.down_z))
+    up_steps = (r.up_grad, (upper, distant_half, side), (far, mirrored, beside), (r.up_y, r.up_z, r.up_x))
+    out_steps = (r.out_piece, (odd, distant_half, side), (ahead, mirrored, beside), (r.out_a, r.out_z, r.out_x))
+
+    def give(steps, at):
+        grad, mine, where, got = steps
+        index = mine[:at] + (1 - mine[at],)
+        if at == 0:
+            source = grad.at[index[0]]
+        elif at == 1:
+            source = grad.at[index[0], index[1]]
+        else:
+            source = grad.at[index[0], index[1], index[2]]
+        return wires.send(source, got[at], where[at])
+
+    def take(steps, at, copy):
+        grad, mine, _, got = steps
+        copy.wait_recv()
+        if at == 0:
+            grad[mine[0]] = rounded(grad[mine[0]].astype(f32) + got[0][...].astype(f32))
+        elif at == 1:
+            grad[mine[0], mine[1]] = rounded(
+                grad[mine[0], mine[1]].astype(f32) + got[1][...].astype(f32)
+            )
+        else:
+            return grad[mine[0], mine[1], mine[2]].astype(f32) + got[2][...].astype(f32)
 
     flat_cot = r.cots[...].reshape(4 * own, model)
     flat_act = r.act[...].reshape(4 * own, ff)
     grads = rounded(contract_rows(flat_cot, flat_act))
     narrow = model // ctx_size
     for at in range(ctx_size):
-        r.down_grad[at % 2, at // 2] = grads[at * narrow : (at + 1) * narrow]
-    down_side = wires.send(r.down_grad.at[1 - side], r.down_side, beside)
+        r.down_grad[at // 2 % 2, at % 2, at // 4] = grads[at * narrow : (at + 1) * narrow]
+    down_y = give(down_steps, 0)
     out_core, out_far_core = (
         wires.later(r.out_part.at[1], r.out_got.at[0], core),
         wires.later(r.out_part.at[3], r.out_got.at[1], core),
@@ -829,10 +850,9 @@
 
     lax.fori_loop(0, 4, out_step, 0)
     flat_grad = r.grad_hid[...].reshape(4 * own, ff)
-    vec_rows = 4 + ff // model
     d_bias_up = jnp.sum(flat_grad.astype(f32), axis=0, keepdims=True)
-    for at in range(ff // model):
-        r.vec[4 + at : 5 + at, :] = d_bias_up[:, at * model : (at + 1) * model]
+    for at in range(4):
+        r.vec[4 + at : 5 + at, :] = jnp.where(ff_block == at, d_bias_up, 0.0)
     flat_normed = r.normed[...].reshape(4 * own, model)
     size = model // 4
     for at in range(shards):
@@ -840,14 +860,12 @@
             contract_rows(flat_normed, flat_grad[:, at * ff // shards : (at + 1) * ff // shards])
         )
         for row in range(4):
-            index = at * 4 + row
-            r.up_grad[index % 2, index // 2] = grads[row * size : (row + 1) * size]
+            r.up_grad[row // 2, row % 2, at] = grads[row * size : (row + 1) * size]
     out_far_core.wait_recv()
     r.out_part[2] = rounded(r.out_part[2].astype(f32) + r.out_got[1].astype(f32))
 
     part_core.wait_recv()
     part_far.wait_recv()
-    out_far = wires.send(r.out_part.at[2], r.out_got.at[2], far)
     grad_normed = r.part[0].astype(f32) + r.part_got[0].astype(f32) + r.part_got[2].astype(f32)
     xhat = r.hat_two[...]
     r.vec[2:3, :] = jnp.sum(grad_normed * xhat, axis=0, keepdims=True)
@@ -865,6 +883,7 @@
         peer = lax.rem(ctx + step, ctx_size)
         att_in.append(wires.send(r.att_out.at[peer], r.grad_in.at[ctx], {"ctx": peer}))
     r.grad_in[ctx] = r.att_out[ctx]
+    up_y = give(up_steps, 0)
     for group in range(groups):
         total = None
         for micro in range(mbs):
@@ -874,19 +893,22 @@
             total = some if total is None else total + some
         total = rounded(total)
         for at in range(ctx_size):
-            r.out_grad[group, at % 2, at // 2] = folded(total[at * narrow : (at + 1) * narrow])
+            r.out_grad[group, at // 2 % 2, at // 4, at % 2] = folded(
+                total[at * narrow : (at + 1) * narrow]
+            )
     out_grad_core = wires.send(r.out_grad.at[swap(dp)], r.out_grad_got.at[0], core)
     out_grad_far_core = wires.send(
         r.out_grad.at[lax.rem(swap(dp) + 2, 4)], r.out_grad_got.at[1], core
     )
+    take(down_steps, 0, down_y)
+    down_x = give(down_steps, 1)
+    for copy in att_in:
+        copy.wait_recv()
+    out_far = wires.send(r.out_part.at[2], r.out_got.at[2], ahead)
     out_grad_far_core.wait_recv()
     mine = lax.rem(dp + 2, 4)
     r.out_grad[mine] = rounded(r.out_grad[mine].astype(f32) + r.out_grad_got[1].astype(f32))
     out_grad_far = wires.send(r.out_grad.at[mine], r.out_grad_got.at[2], far)
-    up_side = wires.send(r.up_grad.at[1 - side], r.up_side, beside)
-    start_line(down_refs, down_side, r.down_side)
-    for copy in att_in:
-        copy.wait_recv()
     for place in range(ctx_size):
         r.grad_att[place] = unfolded(r.grad_in[place])
 
@@ -976,9 +998,11 @@
         r.one_ready[at] = rounded(r.one_own[at] + r.one_side[at].astype(f32))
         near, shared = to_near(at), to_collect(at)
 
-        @pl.when((pair == at // 2) & (line != at))
-        def _():
-            near.start()
+        if at != 2:
+
+            @pl.when((pair == at // 2) & (line != at))
+            def _():
+                near.start()
 
         @pl.when((pair != at // 2) & jnp.logical_not(collects))
         def _():
@@ -999,26 +1023,15 @@
     finish_block(3)
     back_block(2 * block)
     finish_block(2)
-    line_collect(*down_refs)
-    start_line(up_refs, up_side, r.up_side)
+    take(down_steps, 1, down_x)
+    down_z = give(down_steps, 2)
+    take(up_steps, 0, up_y)
+    up_z = give(up_steps, 1)
     back_block(block)
     finish_block(1)
     pass_on(3)
     back_block(0)
     finish_block(0)
-    vec_in = []
-    for step in range(1, ctx_size):
-        peer = lax.rem(ctx + step, ctx_size)
-        vec_in.append(wires.send(r.vec, r.vec_got.at[ctx], {"ctx": peer}))
-    r.vec_got[ctx] = r.vec[...]
-    out_grad_core.wait_recv()
-    out_grad_far.wait_recv()
-    r.out_piece[...] = rounded(
-        r.out_grad[dp].astype(f32)
-        + r.out_grad_got[0].astype(f32)
-        + r.out_grad_got[2].astype(f32)
-    )
-    out_side = wires.send(r.out_piece.at[1 - side], r.out_side, beside)
 
     size = model // 4
     part = math.gcd(width, 3 * model // ctx_size)
@@ -1046,7 +1059,6 @@
         grads_q,
         [(at * part, at * folded_part, part) for at in range(per)] + [(width, tail, HD)],
     )
-    pass_on(2)
     grads_kv = rounded(matmul(rounded(r.acc[...]), r.normed_one[...]))
     store_qkv(
         grads_kv,
@@ -1055,54 +1067,37 @@
     )
     qkv_far_core = wires.send(r.qkv_grad.at[lax.rem(swap(dp) + 2, 4)], r.qkv_got.at[1], core)
     qkv_core = wires.send(r.qkv_grad.at[swap(dp)], r.qkv_got.at[0], core)
-    collect(3)
-    line_collect(*up_refs)
-    pass_on(1)
+    out_grad_core.wait_recv()
+    out_grad_far.wait_recv()
+    r.out_piece[...] = rounded(
+        r.out_grad[dp].astype(f32)
+        + r.out_grad_got[0].astype(f32)
+        + r.out_grad_got[2].astype(f32)
+    )
+    out_a = give(out_steps, 0)
+    for row in range(8):
+        r.vec_rows[row] = r.vec[row : row + 1, :]
+    vec_in = []
+    for step in range(1, ctx_size):
+        peer = lax.rem(ctx + step, ctx_size)
+        vec_in.append(wires.send(r.vec_rows.at[peer], r.vec_got.at[ctx], {"ctx": peer}))
+    r.vec_got[ctx] = r.vec_rows[ctx]
+    pass_on(2)
     qkv_far_core.wait_recv()
     r.qkv_grad[mine] = rounded(r.qkv_grad[mine].astype(f32) + r.qkv_got[1].astype(f32))
     qkv_far = wires.send(r.qkv_grad.at[mine], r.qkv_got.at[2], far)
+    collect(3)
+    pass_on(1)
+    pass_on(0)
+    near_two = to_near(2)
+
+    @pl.when(line == 3)
+    def _():
+        near_two.start()
+
+    take(up_steps, 1, up_z)
+    up_x = give(up_steps, 2)
     collect(2)
-    pass_on(0)
-    collect(1)
-    start_line(out_refs, out_side, r.out_side)
-    collect(0)
-    line_collect(*out_refs)
-    r.d_down[...] = line_finish(*down_refs)
-    out_core.wait_recv()
-    out_far.wait_recv()
-    r.layer[...] = rounded(
-        r.mid[...]
-        + (r.out_part[0].astype(f32) + r.out_got[0].astype(f32) + r.out_got[2].astype(f32))
-    )
-    r.up_sum[...] = rounded(line_finish(*up_refs))
-    stays = (lax.rem(ctx, 4) == dp) & (shards * dp + ctx // 4 == ctx)
-    up_copy = pltpu.make_async_remote_copy(
-        src_ref=r.up_sum,
-        dst_ref=r.up_final,
-        send_sem=r.up_send.at[0],
-        recv_sem=r.up_recv.at[0],
-        device_id=up_to,
-        device_id_type=MESH,
-    )
-
-    @pl.when(jnp.logical_not(stays))
-    def _():
-        up_copy.start()
-
-    @pl.when(stays)
-    def _():
-        r.up_final[...] = r.up_sum[...]
-
-    for copy in vec_in:
-        copy.wait_recv()
-    total = r.vec_got[0]
-    for at in range(1, ctx_size):
-        total += r.vec_got[at]
-    r.vec_sum[...] = total
-    vec_out = [
-        wires.send(r.vec_sum, r.vecs.at[dp], where) for where in (core, far, far_core)
-    ]
-    r.vecs[dp] = total
     qkv_core.wait_recv()
     qkv_far.wait_recv()
     r.qkv_sum[...] = rounded(
@@ -1161,6 +1156,70 @@
                 tail + kind * folded_head : tail + (kind + 1) * folded_head, :
             ]
 
+    collect(1)
+    collect(0)
+    take(out_steps, 0, out_a)
+    out_z = give(out_steps, 1)
+    for copy in vec_in:
+        copy.wait_recv()
+    total = r.vec_got[0]
+    for at in range(1, ctx_size):
+        total += r.vec_got[at]
+    r.vec_sum[...] = total
+    vec_out = [
+        wires.send(r.vec_sum, r.vecs.at[dp], where) for where in (core, far, far_core)
+    ]
+    r.vecs[dp] = total
+    for copy in vec_out:
+        copy.wait_recv()
+    r.vec_total[...] = (r.vecs[0] + r.vecs[1]) + (r.vecs[2] + r.vecs[3])
+    vec_all = [wires.send(r.vec_total, r.vec_last.at[ctx], where) for where in around]
+    r.vec_last[ctx] = r.vec_total[...]
+    r.down_sum[...] = rounded(take(down_steps, 2, down_z))
+    down_final = pltpu.make_async_remote_copy(
+        src_ref=r.down_sum,
+        dst_ref=r.down_final,
+        send_sem=r.up_send.at[1],
+        recv_sem=r.up_recv.at[1],
+        device_id=across,
+        device_id_type=MESH,
+    )
+
+    @pl.when(jnp.logical_not(owns_block))
+    def _():
+        down_final.start()
+
+    @pl.when(owns_block)
+    def _():
+        r.down_final[...] = r.down_sum[...]
+
+    out_core.wait_recv()
+    out_far.wait_recv()
+    r.layer[...] = rounded(
+        r.mid[...]
+        + (r.out_part[0].astype(f32) + r.out_got[0].astype(f32) + r.out_got[2].astype(f32))
+    )
+    r.up_sum[...] = rounded(take(up_steps, 2, up_x))
+    stays = (2 * upper + distant_half == dp) & (2 * ff_block + side == ctx)
+    up_copy = pltpu.make_async_remote_copy(
+        src_ref=r.up_sum,
+        dst_ref=r.up_final,
+        send_sem=r.up_send.at[0],
+        recv_sem=r.up_recv.at[0],
+        device_id=up_to,
+        device_id_type=MESH,
+    )
+
+    @pl.when(jnp.logical_not(stays))
+    def _():
+        up_copy.start()
+
+    @pl.when(stays)
+    def _():
+        r.up_final[...] = r.up_sum[...]
+
+    take(out_steps, 1, out_z)
+    out_x = give(out_steps, 2)
     xhat, inverse_one = norm_parts(r.x[...].astype(f32))
     arrived(r.one_ready.at[0], r.one_near, r.one_recv.at[0])
     arrived(r.one_ready.at[0], r.one_far, r.one_recv.at[1])
@@ -1172,7 +1231,7 @@
         r.d_x[rows, :] = rounded(
             r.grad_mid[rows, :] + norm_back(xhat[rows], inverse_one[rows], grad, gain_one)
         )
-    r.d_out[...] = unfolded(line_finish(*out_refs)).T
+    r.d_out[...] = unfolded(take(out_steps, 2, out_x)).T
 
     @pl.when(jnp.logical_not(stays))
     def _():
@@ -1180,6 +1239,17 @@
         up_copy.wait_recv()
 
     r.d_up[...] = r.up_final[...].astype(f32)
+
+    @pl.when(jnp.logical_not(owns_block))
+    def _():
+        down_final.wait_send()
+        down_final.wait_recv()
+
+    @pl.when(owns_block)
+    def _():
+        down_copy.wait_send()
+
+    r.d_down[...] = r.down_final[...].astype(f32)
 
     for kind in range(3):
         for half in range(per):
@@ -1227,17 +1297,12 @@
             r.deal_sum[slot * part : slot * part + HD, :] += unfolded(total)
 
     r.d_qkv[...] = r.deal_sum[...].T
-    for copy in vec_out:
+    for copy in vec_all:
         copy.wait_recv()
     for row in range(4):
-        r.d_vec[row : row + 1, :] = (
-            r.vecs[0, row : row + 1, :] + r.vecs[1, row : row + 1, :]
-        ) + (r.vecs[2, row : row + 1, :] + r.vecs[3, row : row + 1, :])
-    for at in range(4):
-        r.d_bias[at] = r.vecs[at, 4:vec_rows, :]
+        r.d_vec[row : row + 1, :] = r.vec_last[row]
+        r.d_bias[row] = r.vec_last[4 + row]
     wires.drain()
-    for refs in (down_refs, up_refs, out_refs):
-        line_drain(*refs)
     for place in range(ctx_size):
         copy = att_copy(place)
 
@@ -1253,10 +1318,10 @@
             copy.wait_send()
 
 
-LAYER_COPIES = 96
-
-
-def layer(collective_id, groups, shards, lengths, large):
+LAYER_COPIES = 112
+
+
+def layer(collective_id, groups, shards, lengths, w_down, large):
     bf16, f32 = jnp.bfloat16, jnp.float32
     own, model = large["x"].shape
     ctx_size = lax.axis_size("ctx")
@@ -1265,12 +1330,12 @@
     width = hpg * HD
     row_length = ctx_size * tokens
     lines = ctx_size // 2
-    ff = large["w_down"].shape[0]
+    ff = w_down.shape[0]
     size, shard = model // 4, 3 * model // ctx_size
     part = math.gcd(width, shard)
     slots, mbs = shard // part, ctx_size // groups
     picked = 3 * width + 2 * HD
-    vec_rows = 4 + ff // model
+    vec_rows = 8
     narrow = model // ctx_size
     vmem = pl.BlockSpec(memory_space=pltpu.VMEM)
     anywhere = pl.BlockSpec(memory_space=pl.ANY)
@@ -1313,25 +1378,25 @@
         att_out=((ctx_size, tokens // 2, 2 * width), bf16),
         grad_in=((ctx_size, tokens // 2, 2 * width), bf16),
         grad_att=((ctx_size, tokens, width), bf16),
-        down_grad=((2, lines, narrow, ff), bf16),
-        down_side=((lines, narrow, ff), bf16),
-        down_near=((narrow, ff), bf16),
-        down_distant=((narrow, ff), bf16),
-        down_shared=((2, narrow, ff), bf16),
-        up_grad=((2, lines, size, ff // shards), bf16),
-        up_side=((lines, size, ff // shards), bf16),
-        up_near=((size, ff // shards), bf16),
-        up_distant=((size, ff // shards), bf16),
-        up_shared=((2, size, ff // shards), bf16),
+        down_grad=((2, 2, 2, narrow, ff), bf16),
+        down_y=((2, 2, narrow, ff), bf16),
+        down_x=((2, narrow, ff), bf16),
+        down_z=((narrow, ff), bf16),
+        up_grad=((2, 2, 2, size, ff // shards), bf16),
+        up_y=((2, 2, size, ff // shards), bf16),
+        up_z=((2, size, ff // shards), bf16),
+        up_x=((size, ff // shards), bf16),
         up_sum=((size, ff // shards), bf16),
         up_final=((size, ff // shards), bf16),
-        out_grad=((4, 2, lines, narrow // 2, 2 * size), bf16),
-        out_grad_got=((3, 2, lines, narrow // 2, 2 * size), bf16),
-        out_piece=((2, lines, narrow // 2, 2 * size), bf16),
-        out_side=((lines, narrow // 2, 2 * size), bf16),
-        out_near=((narrow // 2, 2 * size), bf16),
-        out_distant=((narrow // 2, 2 * size), bf16),
-        out_shared=((2, narrow // 2, 2 * size), bf16),
+        down_sum=((narrow, ff), bf16),
+        down_final=((narrow, ff), bf16),
+        w_ff=(w_down.shape, bf16),
+        out_grad=((4, 2, 2, 2, narrow // 2, 2 * size), bf16),
+        out_grad_got=((3, 2, 2, 2, narrow // 2, 2 * size), bf16),
+        out_piece=((2, 2, 2, narrow // 2, 2 * size), bf16),
+        out_a=((2, 2, narrow // 2, 2 * size), bf16),
+        out_z=((2, narrow // 2, 2 * size), bf16),
+        out_x=((narrow // 2, 2 * size), bf16),
         suffix=((1, row_length), f32),
         acc=((2 * width + HD, row_length), f32),
         grad_proj=((row_length, picked), bf16),
@@ -1349,9 +1414,12 @@
         deal_sum=((shard, size), f32),
         extra_got=((ctx_size, HD // 2, 2 * size), bf16),
         vec=((vec_rows, model), f32),
-        vec_got=((ctx_size, vec_rows, model), f32),
-        vec_sum=((vec_rows, model), f32),
-        vecs=((4, vec_rows, model), f32),
+        vec_rows=((vec_rows, 1, model), f32),
+        vec_got=((ctx_size, 1, model), f32),
+        vec_sum=((1, model), f32),
+        vecs=((4, 1, model), f32),
+        vec_total=((1, model), f32),
+        vec_last=((ctx_size, 1, model), f32),
     )
     for start in range(0, row_length, QUERY_BLOCK):
         reach = start + QUERY_BLOCK
@@ -1366,10 +1434,9 @@
         att_recv=dma((ctx_size,)),
         one_send=dma((lines,)),
         one_recv=dma((4,)),
-        line_send=dma((3, 3)),
-        line_recv=dma((3, 3)),
-        up_send=dma((1,)),
-        up_recv=dma((1,)),
+        ff_sem=dma((3,)),
+        up_send=dma((2,)),
+        up_recv=dma((2,)),
         deal_send=dma((3 * (width // part),)),
         deal_recv=dma((slots, mbs)),
         extra_send=dma((2,)),
@@ -1379,14 +1446,14 @@
     return pl.pallas_call(
         partial(layer_body, (groups, shards), list(large), names),
         out_shape=[jax.ShapeDtypeStruct(*spec) for spec in outs.values()],
-        in_specs=[pl.BlockSpec(memory_space=pltpu.SMEM)] + [anywhere] * len(large),
+        in_specs=[pl.BlockSpec(memory_space=pltpu.SMEM)] + [anywhere] * (1 + len(large)),
         out_specs=[vmem] * len(outs),
         scratch_shapes=[pltpu.VMEM(*spec) for spec in scratch.values()] + list(sems.values()),
         compiler_params=pltpu.CompilerParams(
             collective_id=collective_id, has_side_effects=True, vmem_limit_bytes=63 * 1024 * 1024
         ),
         name="layer",
-    )(lengths, *large.values())
+    )(lengths, w_down, *large.values())
 
 
 def finish_body(*refs):
@@ -1442,11 +1509,10 @@
         w_up_own=w_up,
         gain_two=ln2_gain,
         bias_two=ln2_bias,
-        w_down=w_down,
         b_up=b_up,
     )
     layer_out, d_x, d_vec, d_bias, d_qkv, d_out, d_up, d_down = layer(
-        0, ctx_size // mbs, ctx_size // dp_size, doc_lengths, large
+        0, ctx_size // mbs, ctx_size // dp_size, doc_lengths, w_down, large
     )
     layer_out, d_x, d_qkv, d_out, d_up, d_down, gain_one, bias_one, gain_two, bias_two, d_bias = finish(
         layer_out, d_x, d_qkv, d_out, d_up, d_down, d_vec, d_bias
@@ -1478,6 +1544,7 @@
         and ctx_size % dp_size == 0
         and ctx_size == 8
         and mbs == 2
+        and arguments[9].shape[0] == 4 * model
         and (layer_input.shape[2] * ctx_size) % QUERY_BLOCK == 0
     )
     return (per_head_device if fits else per_token_device)(*arguments)

time: 150 us -> 141 us (0.940)
  Pallas kernels: 149 us -> 140 us
    pallas_call x1, Pallas kernels: 147 us -> 137 us  [layer(): pl.pallas_call(partial(layer_body, (groups, shards), list(large), names),...]
where the time goes in v1:
time: 141 us
  Pallas kernels  140 us (99%)
    pallas_call x1, Pallas kernels, layer(): pl.pallas_call(partial(layer_body, (groups, shards), list(large), names),...  137 us

profile of v1, /device:TPU:0, one launch (start us, length us, event | category | flops | bytes accessed | tf_op | source)
XLA Modules:
  0.0 141.0 jit_solution(1803523362363327482)
XLA Ops:
  0.6 137.5 %layer.1 = (bf16[256,768]{1,0:T(8,128)(2,1)}, bf16[256,768]{1,0:T(8,128)(2,1)}, f32[4,768]{1,0:T(4,128)}, f32[4,1,768]{2,1,0:T(1,128)}, f32[192,288]{1,0:T(8,128...) custom-call(s32[2,1,5]{2,1,0:T(1,128)} %lengths.1, bf16[768,768]{1,0:T(8,128)(2,1)} %w_down.1, ...), custom_call_target="tpu_custom_call" | custom-call | tf_op jit(solution)/shard_map/layer/pallas_call | solution.py:1446
  138.1 2.7 %finish.1 = (bf16[256,768]{1,0:T(8,128)(2,1)}, bf16[256,768]{1,0:T(8,128)(2,1)}, f32[192,288]{1,0:T(8,128)}, f32[192,96]{1,0:T(8,128)}, f32[192,384]{1,0:T(8,128...) custom-call(bf16[256,768]{1,0:T(8,128)(2,1)} %get-tuple-element.30.r, ...), custom_call_target="tpu_custom_call" | custom-call | tf_op jit(solution)/shard_map/finish/pallas_call | solution.py:1475

commit v2 on v1

--- a/solution.py
+++ b/solution.py
@@ -500,6 +500,16 @@
     loads.x.wait()
     loads.w_qkv.wait()
     pl.semaphore_wait(barrier, ctx_size + 4)
+
+    flushed = []
+
+    def flush(name):
+        at = len(flushed)
+        copy = pltpu.make_async_copy(
+            getattr(r, name), getattr(r, name + "_hbm"), r.out_sem.at[at]
+        )
+        copy.start()
+        flushed.append(copy)
 
     def x_of(micro):
         return r.x.at[pl.ds(pl.multiple_of(micro * tokens, tokens), tokens)]
@@ -1199,6 +1209,7 @@
         r.mid[...]
         + (r.out_part[0].astype(f32) + r.out_got[0].astype(f32) + r.out_got[2].astype(f32))
     )
+    flush("layer")
     r.up_sum[...] = rounded(take(up_steps, 2, up_x))
     stays = (2 * upper + distant_half == dp) & (2 * ff_block + side == ctx)
     up_copy = pltpu.make_async_remote_copy(
@@ -1231,7 +1242,9 @@
         r.d_x[rows, :] = rounded(
             r.grad_mid[rows, :] + norm_back(xhat[rows], inverse_one[rows], grad, gain_one)
         )
+    flush("d_x")
     r.d_out[...] = unfolded(take(out_steps, 2, out_x)).T
+    flush("d_out")
 
     @pl.when(jnp.logical_not(stays))
     def _():
@@ -1239,6 +1252,7 @@
         up_copy.wait_recv()
 
     r.d_up[...] = r.up_final[...].astype(f32)
+    flush("d_up")
 
     @pl.when(jnp.logical_not(owns_block))
     def _():
@@ -1250,6 +1264,7 @@
         down_copy.wait_send()
 
     r.d_down[...] = r.down_final[...].astype(f32)
+    flush("d_down")
 
     for kind in range(3):
         for half in range(per):
@@ -1297,11 +1312,14 @@
             r.deal_sum[slot * part : slot * part + HD, :] += unfolded(total)
 
     r.d_qkv[...] = r.deal_sum[...].T
+    flush("d_qkv")
     for copy in vec_all:
         copy.wait_recv()
     for row in range(4):
         r.d_vec[row : row + 1, :] = r.vec_last[row]
         r.d_bias[row] = r.vec_last[4 + row]
+    flush("d_vec")
+    flush("d_bias")
     wires.drain()
     for place in range(ctx_size):
         copy = att_copy(place)
@@ -1317,8 +1335,11 @@
         def _():
             copy.wait_send()
 
-
-LAYER_COPIES = 112
+    for copy in flushed:
+        copy.wait()
+
+
+LAYER_COPIES = 76
 
 
 def layer(collective_id, groups, shards, lengths, w_down, large):
@@ -1434,6 +1455,7 @@
         att_recv=dma((ctx_size,)),
         one_send=dma((lines,)),
         one_recv=dma((4,)),
+        out_sem=dma((len(outs),)),
         ff_sem=dma((3,)),
         up_send=dma((2,)),
         up_recv=dma((2,)),
@@ -1442,12 +1464,13 @@
         extra_send=dma((2,)),
         extra_recv=dma((ctx_size,)),
     )
-    names = list(outs) + list(scratch) + list(sems)
+    names = [name + "_hbm" for name in outs] + list(outs) + list(scratch) + list(sems)
+    scratch = outs | scratch
     return pl.pallas_call(
         partial(layer_body, (groups, shards), list(large), names),
         out_shape=[jax.ShapeDtypeStruct(*spec) for spec in outs.values()],
         in_specs=[pl.BlockSpec(memory_space=pltpu.SMEM)] + [anywhere] * (1 + len(large)),
-        out_specs=[vmem] * len(outs),
+        out_specs=[anywhere] * len(outs),
         scratch_shapes=[pltpu.VMEM(*spec) for spec in scratch.values()] + list(sems.values()),
         compiler_params=pltpu.CompilerParams(
             collective_id=collective_id, has_side_effects=True, vmem_limit_bytes=63 * 1024 * 1024

time: 141 us -> 140 us (level)
  no operation moved by 1% of the time
where the time goes in v2:
time: 140 us
  Pallas kernels  139 us (99%)
    pallas_call x1, Pallas kernels, layer(): pl.pallas_call(partial(layer_body, (groups, shards), list(large), names),...  136 us

profile of v2, /device:TPU:0, one launch (start us, length us, event | category | flops | bytes accessed | tf_op | source)
XLA Modules:
  0.0 139.7 jit_solution(851721494902978598)
XLA Ops:
  0.6 136.1 %layer.1 = (bf16[256,768]{1,0:T(8,128)(2,1)}, bf16[256,768]{1,0:T(8,128)(2,1)}, f32[4,768]{1,0:T(4,128)}, f32[4,1,768]{2,1,0:T(1,128)}, f32[192,288]{1,0:T(8,128...) custom-call(s32[2,1,5]{2,1,0:T(1,128)} %lengths.1, bf16[768,768]{1,0:T(8,128)(2,1)} %w_down.1, ...), custom_call_target="tpu_custom_call" | custom-call | tf_op jit(solution)/shard_map/layer/pallas_call | solution.py:1469
  136.8 2.7 %finish.1 = (bf16[256,768]{1,0:T(8,128)(2,1)}, bf16[256,768]{1,0:T(8,128)(2,1)}, f32[192,288]{1,0:T(8,128)}, f32[192,96]{1,0:T(8,128)}, f32[192,384]{1,0:T(8,128...) custom-call(bf16[256,768]{1,0:T(8,128)(2,1)} %get-tuple-element.30.r, ...), custom_call_target="tpu_custom_call" | custom-call | tf_op jit(solution)/shard_map/finish/pallas_call | solution.py:1498
